TPU v7x, 256 devices: a whole 4x4x8 slice. The times are simulated.
256 devices in a mesh: vrow: 16 (over z, core), vcol: 8 (over y, x_lo), pair: 2 (over x_hi).
Axes of the slice: x: 4 (x_hi: 2, x_lo: 2; x = x_hi * 2 + x_lo), y: 4, z: 8, core: 2. Of those that a mesh axis runs over, the one named last changes fastest.
Arguments:
- vertex: bfloat16 [1024, 1024, 500], P('vrow', 'vcol'), may hold values from -0.125 to 0.125
- amps: bfloat16 [192, 8, 1024], P('pair', None, 'vcol'), may hold values from -6 to 6
Outputs:
- ladder: float32 [192, 1024, 1024], P('pair', ('vrow', 'vcol'))
All inputs are finite; a program needn't handle non-finite values.
Results may differ from a plain program's by a relative error of at most 0.0029.
Values may be sent and summed in bfloat16 or wider, within the bound.
No kernel may reach another device: no remote copies, remote signals or barrier semaphores. Data moves between devices by JAX's collectives and lax.ppermute only.
A program may use at most 128 MiB of HBM per device.

v0:
```python
import jax
import jax.numpy as jnp
from jax import lax
from jax.sharding import PartitionSpec as P

NC = 8


def per_device(vertex, amps):
    amp_full = lax.all_gather(amps, "vcol", axis=2, tiled=True)
    vertex_rows = lax.all_to_all(vertex, "vcol", split_axis=0, concat_axis=1, tiled=True)
    inner_terms = lax.dot_general(
        amp_full, vertex_rows, (((2,), (1,)), ((), ())), preferred_element_type=jnp.float32
    ).astype(jnp.bfloat16)
    return lax.dot_general(
        inner_terms,
        lax.all_gather(vertex_rows[:, :NC, :], ("vrow", "vcol"), axis=0, tiled=True),
        (((1, 3), (1, 2)), ((), ())),
        preferred_element_type=jnp.float32,
    )


def solution(mesh):
    placed = (P("vrow", "vcol", None), P("pair", None, "vcol"))
    return jax.shard_map(
        per_device,
        mesh=mesh,
        in_specs=placed,
        out_specs=P("pair", ("vrow", "vcol"), None),
        check_vma=False,
    )
```

profile of v0, /device:TPU:18, one launch (start us, length us, event | category | flops | bytes accessed | tf_op | source)
XLA Modules:
  0.0 544.1 jit_solution(10667512802408852162)
XLA Ops:
  6.5 11.8 %copy.4 = bf16[64,128,500]{1,2,0:T(8,128)(2,1)} copy(bf16[64,128,500]{1,0,2:T(8,128)(2,1)} %param.2) | data formatting | bytes 16384000 | tf_op args[0]
  18.3 7.0 %all-to-all-start = ((bf16[64,128,500]{1,2,0:T(8,128)(2,1)}), bf16[64,128,500]{1,2,0:T(8,128)(2,1)}, u32[]{:S(2)}, u32[]{:S(2)}) async-start(bf16[64,128,500]{1,2,0:T(8,128)(2,1)} %copy.4), calls=%async_computation | async-start | bytes 16515072 | tf_op jit(solution)/shard_map/all_to_all | solution.py:11
  25.3 0.0 all-gather.3.cloned.1.call-start
  25.3 0.7 all-gather.3.cloned.1.call-update
  26.0 0.2 all-gather.5.cloned.1.call-start
  26.2 116.8 %all-to-all-done = bf16[64,128,500]{1,2,0:T(8,128)(2,1)} async-done(((bf16[64,128,500]{1,2,0:T(8,128)(2,1)}), bf16[64,128,500]{1,2,0:T(8,128)(2,1)}, u32[]{:S(2)}, u32[]{:S(2)}) %all-to-all-start) | async-done | bytes 8192032 | tf_op jit(solution)/shard_map/all_to_all | solution.py:11
  143.0 12.8 %copy.5 = bf16[8,8,128,500]{3,1,2,0:T(8,128)(2,1)} copy(bf16[8,8,128,500]{2,3,1,0:T(8,128)(2,1)} %bitcast.2) | data formatting | bytes 16384000 | tf_op jit(solution)/shard_map/all_to_all | solution.py:11
  155.8 1.5 slice.4
  157.3 0.0 all-gather.5.cloned.1.call-update
  157.3 0.0 all-gather.3.cloned.1.call-done
  157.3 11.4 %fusion.2 = bf16[96,8,8,500]{3,1,2,0:T(8,128)(2,1)} fusion(bf16[8,1024,500,1]{2,0,1,3:T(8,128)(2,1)} %bitcast.20, bf16[96,8,1024]{2,1,0:T(8,128)(2,1)} %all-gather.3.cloned.1.call-done), kind=kOutput, calls=%fused_computation.3 | convolution fusion | flops 6291456000 | bytes 15908864 | tf_op jit(solution)/shard_map/dot_general | solution.py:12
  168.7 356.0 %all-gather.5.cloned.1.call-done = bf16[1024,8,500]{2,0,1:T(8,128)(2,1)} async-done(((bf16[8,8,500]{2,0,1:T(8,128)(2,1)}), bf16[1024,8,500]{2,0,1:T(8,128)(2,1)}) %all-gather.5.cloned.1.call-update) | async-done | bytes 8192016 | tf_op jit(solution)/shard_map/all_gather | solution.py:17
  524.7 12.6 %fusion.4 = f32[96,8,1024]{2,1,0:T(8,128)} fusion(bf16[1024,8,500]{2,0,1:T(8,128)(2,1)} %all-gather.5.cloned.1.call-done, bf16[96,8,8,500]{3,1,2,0:T(8,128)(2,1)} %fusion.2), kind=kOutput, calls=%fused_computation.5 | convolution fusion | flops 6291456000 | bytes 17481728 | tf_op jit(solution)/shard_map/dot_general | solution.py:15
Async XLA Ops:
  18.3 124.7 %all-to-all-start = ((bf16[64,128,500]{1,2,0:T(8,128)(2,1)}), bf16[64,128,500]{1,2,0:T(8,128)(2,1)}, u32[]{:S(2)}, u32[]{:S(2)}) async-start(bf16[64,128,500]{1,2,0:T(8,128)(2,1)} %copy.4), calls=%async_computation | async-start | bytes 16515072 | tf_op jit(solution)/shard_map/all_to_all | solution.py:11
  25.3 132.0 %all-gather.3.cloned.1.call-start = ((), (), s32[]{:S(2)}) async-start(), calls=%async_computation.1 | async-start | bytes 1769472 | tf_op jit(solution)/shard_map/all_gather | solution.py:10
  26.0 498.7 %all-gather.5.cloned.1.call-start = ((), (), s32[]{:S(2)}) async-start(), calls=%async_computation.2 | async-start | bytes 8454144 | tf_op jit(solution)/shard_map/all_gather | solution.py:17
Sparse Core Ops, SparseCore 0:
  27.8 73.3 all-gather.2
  157.4 367.2 all-gather.4
where the time goes:
time: 553 us; the launch traced here: 544 us
  waiting for transfers between devices  474 us (86%)
  local copies, waits for them, and re-layouts  26 us (5%)
  matrix products  24 us (4%)
  between operations  13.4 us (2%)
  starting transfers between devices  7.18 us (1%)
    all_gather x1, waiting for transfers between devices, per_device(): lax.all_gather(vertex_rows[:, :NC, :], ('vrow', 'vcol'), axis=0, tiled=True)  356 us
    all_to_all x1, waiting for transfers between devices, per_device(): lax.all_to_all(vertex, 'vcol', split_axis=0, concat_axis=1, tiled=True)  117 us
    all_to_all x1, local copies, waits for them, and re-layouts, per_device(): lax.all_to_all(vertex, 'vcol', split_axis=0, concat_axis=1, tiled=True)  12.8 us
    dot_general x1, matrix products, per_device(): lax.dot_general(inner_terms, lax.all_gather(vertex_rows[:, :NC, :], ('vro...  12.6 us
    unnamed x1, local copies, waits for them, and re-layouts  11.8 us
    dot_general x1, matrix products, per_device(): lax.dot_general(amp_full, vertex_rows, (((2,), (1,)), ((), ())), preferre...  11.4 us
  transfers between devices with their start and end apart: 3, of which 2 were waited for; matrix products, arithmetic and copies ran while one was open for 5% of the time, Pallas kernels for 0%

commit v1 on v0

v1 whole, which is shorter than its diff:
```python
import jax
import jax.numpy as jnp
from jax import lax
from jax.experimental import pallas as pl
from jax.experimental.pallas import tpu as pltpu
from jax.sharding import PartitionSpec as P

NC = 8
AXES = ("vrow", "vcol", "pair")
MIB = 1 << 20


def flat(x, y, z, c):
    x, y, z, c = x % 4, y % 4, z % 8, c % 2
    return ((z * 2 + c) * 8 + (y * 2 + x % 2)) * 2 + x // 2


def send(value, move, only=lambda x, y: True):
    pairs = []
    for x in range(4):
        for y in range(4):
            if not only(x, y):
                continue
            for z in range(8):
                for c in range(2):
                    pairs.append((flat(x, y, z, c), flat(*move(x, y, z, c))))
    return lax.ppermute(value, AXES, pairs)


def step(dx=0, dy=0, dz=0, dc=0):
    return lambda x, y, z, c: (x + dx, y + dy, z + dz, c + dc)


def inner_kernel(mine_ref, other_ref, v_ref, out_ref, t_ref):
    core = lax.rem(lax.axis_index("vrow"), 2)
    pair = lax.axis_index("pair")

    @pl.when(pl.program_id(0) == 0)
    def _():
        for src, own in ((mine_ref, core), (other_ref, 1 - core)):
            for j in range(8):
                for k in range(2):
                    kk = lax.rem(pair + k, 2)
                    for c in range(4):
                        t_ref[own * 4 + c, kk, :, j * 128 : (j + 1) * 128] = src[j * 2 + k, c]

    v = jnp.concatenate([v_ref[j, 0] for j in range(8)], axis=-1)
    t = t_ref[...].reshape(NC * 192, 1024)
    prod = lax.dot_general(t, v, (((1,), (1,)), ((), ())), preferred_element_type=jnp.float32)
    out_ref[...] = prod.astype(jnp.bfloat16).reshape(NC, 1, 2, 96, 500)


def inner_terms(mine, other, v):
    nb = v.shape[1]
    return pl.pallas_call(
        inner_kernel,
        grid=(nb,),
        in_specs=[
            pl.BlockSpec((16, 4, 96, 128), lambda b: (0, 0, 0, 0)),
            pl.BlockSpec((16, 4, 96, 128), lambda b: (0, 0, 0, 0)),
            pl.BlockSpec((8, 1, 500, 128), lambda b: (0, b, 0, 0)),
        ],
        out_specs=pl.BlockSpec((NC, 1, 2, 96, 500), lambda b: (0, b, 0, 0, 0)),
        out_shape=jax.ShapeDtypeStruct((NC, nb, 2, 96, 500), jnp.bfloat16),
        scratch_shapes=[pltpu.VMEM((NC, 2, 96, 1024), jnp.bfloat16)],
        compiler_params=pltpu.CompilerParams(vmem_limit_bytes=48 * MIB),
        cost_estimate=pl.CostEstimate(flops=2 * nb * 1536 * 1024 * 512, bytes_accessed=8 * MIB, transcendentals=0),
    )(mine, other, v)


def ladder_kernel(s_ref, a_ref, b_ref, own_ref, far_ref, acc_ref):
    core = lax.rem(lax.axis_index("vrow"), 2)
    rows = s_ref.shape[1] * 192
    total = None
    for i, src in enumerate((a_ref, b_ref)):
        own = core if i == 0 else 1 - core
        for c in range(4):
            lhs = s_ref[own * 4 + c].reshape(rows, 500)
            p = jnp.dot(lhs, src[c], preferred_element_type=jnp.float32)
            total = p if total is None else total + p
    total = total.reshape(s_ref.shape[1], 2, 96, -1)
    own_ref[...] = total[:, 0]
    far_ref[...] = total[:, 1].astype(jnp.bfloat16)


def ladder_part(s, w_own, w_far):
    nb, na = s.shape[1], w_own.shape[2]
    return pl.pallas_call(
        ladder_kernel,
        out_shape=(
            jax.ShapeDtypeStruct((nb, 96, na), jnp.float32),
            jax.ShapeDtypeStruct((nb, 96, na), jnp.bfloat16),
        ),
        scratch_shapes=[pltpu.VMEM((8, 128), jnp.float32)],
        compiler_params=pltpu.CompilerParams(vmem_limit_bytes=48 * MIB),
        cost_estimate=pl.CostEstimate(flops=2 * nb * 192 * 4096 * na, bytes_accessed=8 * MIB, transcendentals=0),
    )(s, w_own, w_far)


def per_device(vertex, amps):
    vrow, vcol, pair = (lax.axis_index(a) for a in AXES)
    z, core = vrow // 2, lax.rem(vrow, 2)
    y, x_lo = vcol // 2, lax.rem(vcol, 2)

    t = jnp.transpose(amps, (1, 0, 2))
    t = lax.dynamic_slice_in_dim(t, core * 4, 4, 0)
    t = jnp.broadcast_to(t[None], (16, 4, 96, 128))
    t_own = lax.all_to_all(t, ("vcol", "pair"), 0, 0, tiled=True)
    t_far = send(t_own, step(dc=1))

    w = jnp.transpose(vertex[:, :NC, :], (1, 2, 0))
    w_keep = lax.dynamic_slice_in_dim(w, core * 4, 4, 0)
    w_give = lax.dynamic_slice_in_dim(w, (1 - core) * 4, 4, 0)
    w_got = send(w_give, step(dc=1))
    w = jnp.where(core == 0, jnp.concatenate([w_keep, w_got], 2), jnp.concatenate([w_got, w_keep], 2))

    v = lax.dynamic_slice_in_dim(vertex.reshape(8, 2, 4, 128, 500), pair, 1, 1)[:, 0]
    v = jnp.transpose(v, (0, 1, 3, 2))
    v = lax.all_to_all(v, "vcol", 0, 0, tiled=True)

    even = lambda x: x % 2 == 0
    up = send(w, step(dy=1), lambda x, y: even(x) and y == 0)
    down = send(w, step(dy=-1), lambda x, y: even(x) and y == 0)
    w = jnp.where(y == 0, w, jnp.where(y == 1, up, down))
    up = send(w[:2], step(dy=1), lambda x, y: even(x) and y == 1)
    down = send(w[2:], step(dy=-1), lambda x, y: even(x) and y == 3)
    w = jnp.where(y == 2, jnp.concatenate([up, down], 0), w)
    up = send(w[:2], step(dx=1), lambda x, y: even(x))
    down = send(w[2:], step(dx=-1), lambda x, y: even(x))
    w = jnp.where(x_lo == 1, jnp.concatenate([up, down], 0), w)

    ups, downs = [w], [w]
    for _ in range(3):
        ups.append(send(ups[-1], step(dz=1)))
        downs.append(send(downs[-1], step(dz=-1)))
    opposite = jnp.concatenate([send(ups[-1][:2], step(dz=1)), send(downs[-1][2:], step(dz=-1))], 0)

    s = inner_terms(t_own, t_far, v)

    parts = [(w, opposite, 0, 4)] + [(ups[i], downs[i], -i, i) for i in (1, 2, 3)]
    order = [None] * 8
    for first, second, d1, d2 in (parts[1], parts[2], parts[3], parts[0]):
        blocks = jnp.concatenate([first, second], 2)
        far = send(blocks, step(dc=1))
        mine, theirs = ladder_part(s, blocks, far)
        got = send(theirs, step(dx=2)).astype(jnp.float32)
        full = jnp.where(pair == 0, jnp.concatenate([mine, got], 0), jnp.concatenate([got, mine], 0))
        full = jnp.transpose(full, (1, 0, 2))
        order[d1 % 8] = full[..., :128]
        order[d2 % 8] = full[..., 128:]
    out = jnp.concatenate(order + order, 2)
    return lax.dynamic_slice_in_dim(out, lax.rem(8 - z, 8) * 128, 1024, 2)


def solution(mesh):
    return jax.shard_map(
        per_device,
        mesh=mesh,
        in_specs=(P("vrow", "vcol", None), P("pair", None, "vcol")),
        out_specs=P("pair", ("vrow", "vcol"), None),
        check_vma=False,
    )
```

time: 553 us -> 244 us (0.44); the launches traced: 544 us -> 243 us
  waiting for transfers between devices: 474 us -> 102 us
  starting transfers between devices: 7.18 us -> 52.5 us
  Pallas kernels: 0 us -> 30.9 us
  local copies, waits for them, and re-layouts: 26 us -> 54.6 us
  matrix products: 24 us -> 0 us
  between operations: 13.4 us -> 0.55 us
    all_gather x2 -> x0, waiting for transfers between devices: 356 us -> none  [the longest x1 356 us: per_device(): lax.all_gather(vertex_rows[:, :NC, :], ('vrow', 'vcol'), axis=0, tiled=True)]
    all_to_all x1 -> x2, waiting for transfers between devices: 117 us -> 0.01 us  [the longest x1 0.01 us: per_device(): v = lax.all_to_all(v, 'vcol', 0, 0, tiled=True)]
    ppermute x0 -> x24, waiting for transfers between devices: none -> 102 us  [send(): return lax.ppermute(value, AXES, pairs)]
    pallas_call x0 -> x5, Pallas kernels: none -> 30.9 us  [the longest x4 19.1 us: ladder_part(): pl.pallas_call(ladder_kernel, out_shape=(jax.ShapeDtypeStruct((nb, 96, na...]
    ppermute x0 -> x24, starting transfers between devices: none -> 29.8 us  [send(): return lax.ppermute(value, AXES, pairs)]
    dot_general x2 -> x0, matrix products: 24 us -> none  [the longest x1 12.6 us: per_device(): lax.dot_general(inner_terms, lax.all_gather(vertex_rows[:, :NC, :], ('vro...]
    all_to_all x1 -> x2, starting transfers between devices: 6.96 us -> 22.7 us  [the longest x1 15.5 us: per_device(): v = lax.all_to_all(v, 'vcol', 0, 0, tiled=True)]
    another operation x0 -> x1, local copies, waits for them, and re-layouts: none -> 14.3 us
  transfers between devices with their start and end apart: 3 -> 26, of which waited for: 2 -> 9; matrix products, arithmetic and copies ran while one was open for 5% -> 21% of each run, Pallas kernels for 0% -> 13%
where the time goes in v1:
time: 244 us; the launch traced here: 243 us
  waiting for transfers between devices  102 us (42%)
  local copies, waits for them, and re-layouts  54.6 us (22%)
  starting transfers between devices  52.5 us (22%)
  Pallas kernels  30.9 us (13%)
  other arithmetic  2.51 us (1%)
    ppermute x24, waiting for transfers between devices, send(): return lax.ppermute(value, AXES, pairs)  102 us
    ppermute x24, starting transfers between devices, send(): return lax.ppermute(value, AXES, pairs)  29.8 us
    pallas_call x4, Pallas kernels, ladder_part(): pl.pallas_call(ladder_kernel, out_shape=(jax.ShapeDtypeStruct((nb, 96, na...  19.1 us
    unnamed x34, local copies, waits for them, and re-layouts  15.5 us
    all_to_all x1, starting transfers between devices, per_device(): v = lax.all_to_all(v, 'vcol', 0, 0, tiled=True)  15.5 us
    another operation x1, local copies, waits for them, and re-layouts  14.3 us
    pallas_call x1, Pallas kernels, inner_terms(): pl.pallas_call(inner_kernel, grid=(nb,), in_specs=[pl.BlockSpec((16, 4, 9...  11.8 us
    all_to_all x1, starting transfers between devices, per_device(): t_own = lax.all_to_all(t, ('vcol', 'pair'), 0, 0, tiled=True)  7.25 us
  transfers between devices with their start and end apart: 26, of which 9 were waited for; matrix products, arithmetic and copies ran while one was open for 21% of the time, Pallas kernels for 13%

profile of v1, /device:TPU:18, one launch (start us, length us, event | category | flops | bytes accessed | tf_op | source)
XLA Modules:
  0.0 243.3 jit_solution(16860758983465890230)
XLA Ops:
  1.0 1.4 broadcast_in_dim.2
  2.5 7.3 %all-to-all-start = ((bf16[16,4,96,128]{3,2,1,0:T(8,128)(2,1)}), bf16[16,4,96,128]{3,2,1,0:T(8,128)(2,1)}, u32[]{:S(2)}, u32[]{:S(2)}) async-start(bf16[16,4,96,128]{3,2,1,0:T(8,128)(2,1)} %broadcast_in_dim.2), calls=%async_computation | async-start | bytes 3145728 | tf_op jit(solution)/shard_map/all_to_all | solution.py:108
  9.7 14.3 %constant_dynamic-slice_fusion.2 = (bf16[64,4,500]{1,0,2:T(8,128)(2,1)}, bf16[64,4,500]{1,0,2:T(8,128)(2,1)}) fusion(bf16[64,8,500]{1,0,2:T(8,128)(2,1)} %bitcast.18, s32[]{:T(128)S(6)} %select_n.74, s32[]{:T(128)S(6)} %select_n.81), kind=kLoop, calls=%fused_computation.39 | loop fusion | bytes 1024008 | tf_op jit(solution)/shard_map/dynamic-slice.1
  24.1 6.8 %copy.23 = bf16[64,4,500]{0,2,1:T(8,128)(2,1)S(1)} copy(bf16[64,4,500]{1,0,2:T(8,128)(2,1)} %get-tuple-element.22) | data formatting | bytes 512000
  30.9 6.8 %copy.22 = bf16[64,4,500]{0,2,1:T(8,128)(2,1)S(1)} copy(bf16[64,4,500]{1,0,2:T(8,128)(2,1)} %get-tuple-element.21) | data formatting | bytes 512000
  39.7 5.6 %copy_bitcast_fusion = bf16[8,4,500,128]{3,1,2,0:T(4,128)(2,1)} fusion(bf16[8,2,4,128,500]{3,2,1,0,4:T(4,128)(2,1)} %bitcast.19, s32[]{:T(128)S(6)} %select_n.75), kind=kLoop, calls=%fused_computation | loop fusion | bytes 8192004 | tf_op jit(solution)/shard_map/transpose | solution.py:118
  45.5 15.5 %all-to-all-start.1 = ((bf16[8,4,500,128]{3,1,2,0:T(4,128)(2,1)}), bf16[8,4,500,128]{3,1,2,0:T(4,128)(2,1)}, u32[]{:S(2)}, u32[]{:S(2)}) async-start(bf16[8,4,500,128]{3,1,2,0:T(4,128)(2,1)} %copy_bitcast_fusion), calls=%async_computation.1 | async-start | bytes 8192000 | tf_op jit(solution)/shard_map/all_to_all | solution.py:119
  65.1 54.5 %collective-permute-done.6 = bf16[2,500,128]{2,1,0:T(8,128)(2,1)S(1)} collective-permute-done((bf16[2,500,128]{2,1,0:T(8,128)(2,1)S(1)}, bf16[2,500,128]{2,1,0:T(8,128)(2,1)S(1)}, u32[]{:S(2)}, u32[]{:S(2)}) %collective-permute-start.6) | collective-permute-done | bytes 256032 | tf_op jit(solution)/shard_map/ppermute | solution.py:27
  119.6 2.2 collective-permute-done.7
  121.9 2.0 collective-permute-start.8
  123.9 4.0 %collective-permute-start.12 = (bf16[4,500,128]{2,1,0:T(8,128)(2,1)S(1)}, bf16[4,500,128]{2,1,0:T(8,128)(2,1)S(1)}, u32[]{:S(2)}, u32[]{:S(2)}) collective-permute-start(bf16[4,500,128]{2,1,0:T(8,128)(2,1)S(1)} %maximum_select_fusion.6), channel_id=1, source_target_pairs={{0,224},{16,240},{32,0},{48,16},{64,32},{80,48},{96,64},{112,80},{... | collective-permute-start | bytes 1536008 | tf_op jit(solution)/shard_map/ppermute | solution.py:27
  127.9 10.2 %collective-permute-done.8 = bf16[4,500,128]{2,1,0:T(8,128)(2,1)S(1)} collective-permute-done((bf16[4,500,128]{2,1,0:T(8,128)(2,1)S(1)}, bf16[4,500,128]{2,1,0:T(8,128)(2,1)S(1)}, u32[]{:S(2)}, u32[]{:S(2)}) %collective-permute-start.8) | collective-permute-done | bytes 512032 | tf_op jit(solution)/shard_map/ppermute | solution.py:27
  138.1 3.2 %collective-permute-start.13 = (bf16[4,500,128]{2,1,0:T(8,128)(2,1)S(1)}, bf16[4,500,128]{2,1,0:T(8,128)(2,1)S(1)}, u32[]{:S(2)}, u32[]{:S(2)}) collective-permute-start(bf16[4,500,128]{2,1,0:T(8,128)(2,1)S(1)} %collective-permute-done.12), channel_id=1, source_target_pairs={{0,224},{16,240},{32,0},{48,16},{64,32},{80,48},{96,64},{112,80},{... | collective-permute-start | bytes 1536008 | tf_op jit(solution)/shard_map/ppermute | solution.py:27
  142.6 8.1 %collective-permute-done.9 = bf16[4,500,128]{2,1,0:T(8,128)(2,1)S(1)} collective-permute-done((bf16[4,500,128]{2,1,0:T(8,128)(2,1)S(1)}, bf16[4,500,128]{2,1,0:T(8,128)(2,1)S(1)}, u32[]{:S(2)}, u32[]{:S(2)}) %collective-permute-start.9) | collective-permute-done | bytes 512032 | tf_op jit(solution)/shard_map/ppermute | solution.py:27
  151.8 3.2 %collective-permute-start.14 = (bf16[4,500,128]{2,1,0:T(8,128)(2,1)S(1)}, bf16[4,500,128]{2,1,0:T(8,128)(2,1)S(1)}, u32[]{:S(2)}, u32[]{:S(2)}) collective-permute-start(bf16[4,500,128]{2,1,0:T(8,128)(2,1)S(1)} %collective-permute-done.13), channel_id=1, source_target_pairs={{0,224},{16,240},{32,0},{48,16},{64,32},{80,48},{96,64},{112,80},{... | collective-permute-start | bytes 1536008 | tf_op jit(solution)/shard_map/ppermute | solution.py:27
  155.0 12.1 %collective-permute-done.10 = bf16[4,500,128]{2,1,0:T(8,128)(2,1)S(1)} collective-permute-done((bf16[4,500,128]{2,1,0:T(8,128)(2,1)S(1)}, bf16[4,500,128]{2,1,0:T(8,128)(2,1)S(1)}, u32[]{:S(2)}, u32[]{:S(2)}) %collective-permute-start.10) | collective-permute-done | bytes 512032 | tf_op jit(solution)/shard_map/ppermute | solution.py:27
  167.2 3.3 %collective-permute-start.15 = (bf16[2,500,128]{2,1,0:T(8,128)(2,1)S(1)}, bf16[2,500,128]{2,1,0:T(8,128)(2,1)S(1)}, u32[]{:S(2)}, u32[]{:S(2)}) collective-permute-start(bf16[2,500,128]{2,1,0:T(8,128)(2,1)S(1)} %slice.65), channel_id=1, source_target_pairs={{0,224},{16,240},{32,0},{48,16},{64,32},{80,48},{96,64},{112,80},{... | collective-permute-start | bytes 768008 | tf_op jit(solution)/shard_map/ppermute | solution.py:27
  170.7 1.4 copy.17
  173.3 2.9 %collective-permute-done.11 = bf16[2,500,128]{2,1,0:T(8,128)(2,1)S(1)} collective-permute-done((bf16[2,500,128]{2,1,0:T(8,128)(2,1)S(1)}, bf16[2,500,128]{2,1,0:T(8,128)(2,1)S(1)}, u32[]{:S(2)}, u32[]{:S(2)}) %collective-permute-start.11) | collective-permute-done | bytes 256032 | tf_op jit(solution)/shard_map/ppermute | solution.py:27
  176.3 1.4 copy.11
  178.8 4.7 %copy.9.v_ref = bf16[8,4,500,128]{3,2,1,0:T(8,128)(2,1)} copy(bf16[8,4,500,128]{3,1,2,0:T(4,128)(2,1)} %all-to-all-done.1) | data formatting | bytes 8192000 | tf_op jit(solution)/shard_map/all_to_all | solution.py:119
  183.5 11.8 %shard_map.28.s_ref = bf16[8,4,2,96,500]{4,3,2,1,0:T(8,128)(2,1)} custom-call(bf16[16,4,96,128]{3,2,1,0:T(8,128)(2,1)} %all-to-all-done.mine_ref, bf16[16,4,96,128]{3,2,1,0:T(8,128)(2,1)} %collective-permute-done.other_ref, bf16[8,4,500,128]{3,2,1,0:T(8,128)(2,1)} %copy.9.v_ref), custom_call_target="tpu_custom_call" | custom-call | flops 6442450944 | bytes 8388608 | tf_op jit(solution)/shard_map/pallas_call | solution.py:55
  195.3 5.4 %shard_map.31 = (f32[4,96,256]{2,1,0:T(8,128)S(1)}, bf16[4,96,256]{2,1,0:T(8,128)(2,1)}) custom-call(bf16[8,4,2,96,500]{4,3,2,1,0:T(8,128)(2,1)} %shard_map.28.s_ref, bf16[4,500,256]{2,1,0:T(8,128)(2,1)S(1)} %constant_dynamic-update-slice_fusion.2.a_ref, bf16[4,500,256]{2,1,0:T(8,128)(2,1)S(1)} %copy-done.5), custom_call_target="tpu_custom_call" | custom-call | flops 1610612736 | bytes 8388608 | tf_op jit(solution)/shard_map/pallas_call | solution.py:88
  201.9 4.6 %shard_map.30 = (f32[4,96,256]{2,1,0:T(8,128)S(1)}, bf16[4,96,256]{2,1,0:T(8,128)(2,1)S(1)}) custom-call(bf16[8,4,2,96,500]{4,3,2,1,0:T(8,128)(2,1)} %shard_map.28.s_ref, bf16[4,500,256]{2,1,0:T(8,128)(2,1)S(1)} %copy-done.3, bf16[4,500,256]{2,1,0:T(8,128)(2,1)S(1)} %copy-done.4), custom_call_target="tpu_custom_call" | custom-call | flops 1610612736 | bytes 8388608 | tf_op jit(solution)/shard_map/pallas_call | solution.py:88
  206.5 2.7 %collective-permute-start.19 = (bf16[4,96,256]{2,1,0:T(8,128)(2,1)S(1)}, bf16[4,96,256]{2,1,0:T(8,128)(2,1)S(1)}, u32[]{:S(2)}, u32[]{:S(2)}) collective-permute-start(bf16[4,96,256]{2,1,0:T(8,128)(2,1)S(1)} %get-tuple-element.16), channel_id=1, source_target_pairs={{0,1},{16,17},{32,33},{48,49},{64,65},{80,81},{96,97},{112,113},{1... | collective-permute-start | bytes 589832 | tf_op jit(solution)/shard_map/ppermute | solution.py:27
  209.8 5.5 %collective-permute-done.19 = bf16[4,96,256]{2,1,0:T(8,128)(2,1)S(1)} collective-permute-done((bf16[4,96,256]{2,1,0:T(8,128)(2,1)S(1)}, bf16[4,96,256]{2,1,0:T(8,128)(2,1)S(1)}, u32[]{:S(2)}, u32[]{:S(2)}) %collective-permute-start.19) | collective-permute-done | bytes 196640 | tf_op jit(solution)/shard_map/ppermute | solution.py:27
  216.6 1.4 copy.18.b_ref
  217.9 4.6 %shard_map.32 = (f32[4,96,256]{2,1,0:T(8,128)S(1)}, bf16[4,96,256]{2,1,0:T(8,128)(2,1)S(1)}) custom-call(bf16[8,4,2,96,500]{4,3,2,1,0:T(8,128)(2,1)} %shard_map.28.s_ref, bf16[4,500,256]{2,1,0:T(8,128)(2,1)S(1)} %constant_dynamic-update-slice_fusion.4.a_ref, bf16[4,500,256]{2,1,0:T(8,128)(2,1)S(1)} %copy.18.b_ref), custom_call_target="tpu_custom_call" | custom-call | flops 1610612736 | bytes 8388608 | tf_op jit(solution)/shard_map/pallas_call | solution.py:88
  222.5 2.5 %collective-permute-start.23 = (bf16[4,96,256]{2,1,0:T(8,128)(2,1)S(1)}, bf16[4,96,256]{2,1,0:T(8,128)(2,1)S(1)}, u32[]{:S(2)}, u32[]{:S(2)}) collective-permute-start(bf16[4,96,256]{2,1,0:T(8,128)(2,1)S(1)} %get-tuple-element.20), channel_id=1, source_target_pairs={{0,1},{16,17},{32,33},{48,49},{64,65},{80,81},{96,97},{112,113},{1... | collective-permute-start | bytes 589832 | tf_op jit(solution)/shard_map/ppermute | solution.py:27
  226.3 4.6 %shard_map.29 = (f32[4,96,256]{2,1,0:T(8,128)S(1)}, bf16[4,96,256]{2,1,0:T(8,128)(2,1)S(1)}) custom-call(bf16[8,4,2,96,500]{4,3,2,1,0:T(8,128)(2,1)} %shard_map.28.s_ref, bf16[4,500,256]{2,1,0:T(8,128)(2,1)S(1)} %maximum_maximum_fusion.a_ref, bf16[4,500,256]{2,1,0:T(8,128)(2,1)S(1)} %copy.12.b_ref), custom_call_target="tpu_custom_call" | custom-call | flops 1610612736 | bytes 8388608 | tf_op jit(solution)/shard_map/pallas_call | solution.py:88
  232.4 6.1 %collective-permute-done.17 = bf16[4,96,256]{2,1,0:T(8,128)(2,1)S(1)} collective-permute-done((bf16[4,96,256]{2,1,0:T(8,128)(2,1)S(1)}, bf16[4,96,256]{2,1,0:T(8,128)(2,1)S(1)}, u32[]{:S(2)}, u32[]{:S(2)}) %collective-permute-start.17) | collective-permute-done | bytes 196640 | tf_op jit(solution)/shard_map/ppermute | solution.py:27
  239.9 3.5 %copy.19 = f32[96,8,1024]{2,1,0:T(8,128)} copy(f32[96,8,1024]{2,0,1:T(8,128)S(1)} %constant_dynamic-slice_fusion) | data formatting | bytes 6291456 | tf_op jit(solution)/shard_map/dynamic_slice | solution.py:152
  (96 shorter events, 19.4 us)
Async XLA Ops:
  2.5 43.0 %all-to-all-start = ((bf16[16,4,96,128]{3,2,1,0:T(8,128)(2,1)}), bf16[16,4,96,128]{3,2,1,0:T(8,128)(2,1)}, u32[]{:S(2)}, u32[]{:S(2)}) async-start(bf16[16,4,96,128]{3,2,1,0:T(8,128)(2,1)} %broadcast_in_dim.2), calls=%async_computation | async-start | bytes 3145728 | tf_op jit(solution)/shard_map/all_to_all | solution.py:108
  30.8 6.9 %collective-permute-start.1 = (bf16[4,500,64]{2,1,0:T(8,128)(2,1)S(1)}, bf16[4,500,64]{2,1,0:T(8,128)(2,1)S(1)}, u32[]{:S(2)}, u32[]{:S(2)}) collective-permute-start(bf16[4,500,64]{2,1,0:T(8,128)(2,1)S(1)} %bitcast.21), channel_id=1, source_target_pairs={{0,16},{16,0},{32,48},{48,32},{64,80},{80,64},{96,112},{112,96},{1... | collective-permute-start | bytes 768008 | tf_op jit(solution)/shard_map/ppermute | solution.py:27
  38.3 7.0 %collective-permute-start.2 = (bf16[4,500,128]{2,1,0:T(8,128)(2,1)S(1)}, bf16[4,500,128]{2,1,0:T(8,128)(2,1)S(1)}, u32[]{:S(2)}, u32[]{:S(2)}) collective-permute-start(bf16[4,500,128]{2,1,0:T(8,128)(2,1)S(1)} %maximum_select_fusion.4), channel_id=1, source_target_pairs={{0,4},{16,20},{32,36},{48,52},{64,68},{80,84},{96,100},{112,116},{... | collective-permute-start | bytes 1536008 | tf_op jit(solution)/shard_map/ppermute | solution.py:27
  39.0 6.3 %collective-permute-start.3 = (bf16[4,500,128]{2,1,0:T(8,128)(2,1)S(1)}, bf16[4,500,128]{2,1,0:T(8,128)(2,1)S(1)}, u32[]{:S(2)}, u32[]{:S(2)}) collective-permute-start(bf16[4,500,128]{2,1,0:T(8,128)(2,1)S(1)} %maximum_select_fusion.4), channel_id=1, source_target_pairs={{0,12},{16,28},{32,44},{48,60},{64,76},{80,92},{96,108},{112,124},... | collective-permute-start | bytes 1536008 | tf_op jit(solution)/shard_map/ppermute | solution.py:27
  45.5 133.3 %all-to-all-start.1 = ((bf16[8,4,500,128]{3,1,2,0:T(4,128)(2,1)}), bf16[8,4,500,128]{3,1,2,0:T(4,128)(2,1)}, u32[]{:S(2)}, u32[]{:S(2)}) async-start(bf16[8,4,500,128]{3,1,2,0:T(4,128)(2,1)} %copy_bitcast_fusion), calls=%async_computation.1 | async-start | bytes 8192000 | tf_op jit(solution)/shard_map/all_to_all | solution.py:119
  61.0 1.4 collective-permute-start.4
  61.6 0.7 collective-permute-start.5
  62.5 57.1 %collective-permute-start.6 = (bf16[2,500,128]{2,1,0:T(8,128)(2,1)S(1)}, bf16[2,500,128]{2,1,0:T(8,128)(2,1)S(1)}, u32[]{:S(2)}, u32[]{:S(2)}) collective-permute-start(bf16[2,500,128]{2,1,0:T(8,128)(2,1)S(1)} %get-tuple-element.23), channel_id=1, source_target_pairs={{0,2},{16,18},{32,34},{48,50},{64,66},{80,82},{96,98},{112,114},{1... | collective-permute-start | bytes 768008 | tf_op jit(solution)/shard_map/ppermute | solution.py:27
  63.8 58.0 %collective-permute-start.7 = (bf16[2,500,128]{2,1,0:T(8,128)(2,1)S(1)}, bf16[2,500,128]{2,1,0:T(8,128)(2,1)S(1)}, u32[]{:S(2)}, u32[]{:S(2)}) collective-permute-start(bf16[2,500,128]{2,1,0:T(8,128)(2,1)S(1)} %get-tuple-element.24), channel_id=1, source_target_pairs={{0,3},{16,19},{32,35},{48,51},{64,67},{80,83},{96,99},{112,115},{1... | collective-permute-start | bytes 768008 | tf_op jit(solution)/shard_map/ppermute | solution.py:27
  121.9 16.2 %collective-permute-start.8 = (bf16[4,500,128]{2,1,0:T(8,128)(2,1)S(1)}, bf16[4,500,128]{2,1,0:T(8,128)(2,1)S(1)}, u32[]{:S(2)}, u32[]{:S(2)}) collective-permute-start(bf16[4,500,128]{2,1,0:T(8,128)(2,1)S(1)} %maximum_select_fusion.6), channel_id=1, source_target_pairs={{0,32},{16,48},{32,64},{48,80},{64,96},{80,112},{96,128},{112,144}... | collective-permute-start | bytes 1536008 | tf_op jit(solution)/shard_map/ppermute | solution.py:27
  123.9 14.3 %collective-permute-start.12 = (bf16[4,500,128]{2,1,0:T(8,128)(2,1)S(1)}, bf16[4,500,128]{2,1,0:T(8,128)(2,1)S(1)}, u32[]{:S(2)}, u32[]{:S(2)}) collective-permute-start(bf16[4,500,128]{2,1,0:T(8,128)(2,1)S(1)} %maximum_select_fusion.6), channel_id=1, source_target_pairs={{0,224},{16,240},{32,0},{48,16},{64,32},{80,48},{96,64},{112,80},{... | collective-permute-start | bytes 1536008 | tf_op jit(solution)/shard_map/ppermute | solution.py:27
  138.1 12.6 %collective-permute-start.9 = (bf16[4,500,128]{2,1,0:T(8,128)(2,1)S(1)}, bf16[4,500,128]{2,1,0:T(8,128)(2,1)S(1)}, u32[]{:S(2)}, u32[]{:S(2)}) collective-permute-start(bf16[4,500,128]{2,1,0:T(8,128)(2,1)S(1)} %collective-permute-done.8), channel_id=1, source_target_pairs={{0,32},{16,48},{32,64},{48,80},{64,96},{80,112},{96,128},{112,144}... | collective-permute-start | bytes 1536008 | tf_op jit(solution)/shard_map/ppermute | solution.py:27
  138.1 12.7 %collective-permute-start.13 = (bf16[4,500,128]{2,1,0:T(8,128)(2,1)S(1)}, bf16[4,500,128]{2,1,0:T(8,128)(2,1)S(1)}, u32[]{:S(2)}, u32[]{:S(2)}) collective-permute-start(bf16[4,500,128]{2,1,0:T(8,128)(2,1)S(1)} %collective-permute-done.12), channel_id=1, source_target_pairs={{0,224},{16,240},{32,0},{48,16},{64,32},{80,48},{96,64},{112,80},{... | collective-permute-start | bytes 1536008 | tf_op jit(solution)/shard_map/ppermute | solution.py:27
  141.4 42.1 %collective-permute-start = (bf16[16,4,96,128]{3,2,1,0:T(8,128)(2,1)}, bf16[16,4,96,128]{3,2,1,0:T(8,128)(2,1)}, u32[]{:S(2)}, u32[]{:S(2)}) collective-permute-start(bf16[16,4,96,128]{3,2,1,0:T(8,128)(2,1)} %all-to-all-done.mine_ref), channel_id=1, source_target_pairs={{0,16},{16,0},{32,48},{48,32},{64,80},{80,64},{96,112},{112,96},{1... | collective-permute-start | bytes 4718600 | tf_op jit(solution)/shard_map/ppermute | solution.py:27
  141.6 31.7 %copy-start.2 = (bf16[4,500,256]{2,1,0:T(8,128)(2,1)}, bf16[4,500,256]{2,1,0:T(8,128)(2,1)S(1)}, u32[]{:S(2)}) copy-start(bf16[4,500,256]{2,1,0:T(8,128)(2,1)S(1)} %constant_dynamic-update-slice_fusion.a_ref) | copy-start | bytes 3072004
  142.0 30.1 %collective-permute-start.18 = (bf16[4,500,256]{2,0,1:T(4,128)(2,1)S(1)}, bf16[4,500,256]{2,0,1:T(4,128)(2,1)S(1)}, u32[]{:S(2)}, u32[]{:S(2)}) collective-permute-start(bf16[4,500,256]{2,0,1:T(4,128)(2,1)S(1)} %copy.13), channel_id=1, source_target_pairs={{0,16},{16,0},{32,48},{48,32},{64,80},{80,64},{96,112},{112,96},{1... | collective-permute-start | bytes 3072008 | tf_op jit(solution)/shard_map/ppermute | solution.py:27
  151.4 26.3 %collective-permute-start.20 = (bf16[4,500,256]{2,0,1:T(4,128)(2,1)S(1)}, bf16[4,500,256]{2,0,1:T(4,128)(2,1)S(1)}, u32[]{:S(2)}, u32[]{:S(2)}) collective-permute-start(bf16[4,500,256]{2,0,1:T(4,128)(2,1)S(1)} %copy.15), channel_id=1, source_target_pairs={{0,16},{16,0},{32,48},{48,32},{64,80},{80,64},{96,112},{112,96},{1... | collective-permute-start | bytes 3072008 | tf_op jit(solution)/shard_map/ppermute | solution.py:27
  151.7 15.4 %collective-permute-start.10 = (bf16[4,500,128]{2,1,0:T(8,128)(2,1)S(1)}, bf16[4,500,128]{2,1,0:T(8,128)(2,1)S(1)}, u32[]{:S(2)}, u32[]{:S(2)}) collective-permute-start(bf16[4,500,128]{2,1,0:T(8,128)(2,1)S(1)} %collective-permute-done.9), channel_id=1, source_target_pairs={{0,32},{16,48},{32,64},{48,80},{64,96},{80,112},{96,128},{112,144}... | collective-permute-start | bytes 1536008 | tf_op jit(solution)/shard_map/ppermute | solution.py:27
  151.8 15.4 %collective-permute-start.14 = (bf16[4,500,128]{2,1,0:T(8,128)(2,1)S(1)}, bf16[4,500,128]{2,1,0:T(8,128)(2,1)S(1)}, u32[]{:S(2)}, u32[]{:S(2)}) collective-permute-start(bf16[4,500,128]{2,1,0:T(8,128)(2,1)S(1)} %collective-permute-done.13), channel_id=1, source_target_pairs={{0,224},{16,240},{32,0},{48,16},{64,32},{80,48},{96,64},{112,80},{... | collective-permute-start | bytes 1536008 | tf_op jit(solution)/shard_map/ppermute | solution.py:27
  167.1 9.1 %collective-permute-start.11 = (bf16[2,500,128]{2,1,0:T(8,128)(2,1)S(1)}, bf16[2,500,128]{2,1,0:T(8,128)(2,1)S(1)}, u32[]{:S(2)}, u32[]{:S(2)}) collective-permute-start(bf16[2,500,128]{2,1,0:T(8,128)(2,1)S(1)} %slice.64), channel_id=1, source_target_pairs={{0,32},{16,48},{32,64},{48,80},{64,96},{80,112},{96,128},{112,144}... | collective-permute-start | bytes 768008 | tf_op jit(solution)/shard_map/ppermute | solution.py:27
  167.2 8.9 %collective-permute-start.15 = (bf16[2,500,128]{2,1,0:T(8,128)(2,1)S(1)}, bf16[2,500,128]{2,1,0:T(8,128)(2,1)S(1)}, u32[]{:S(2)}, u32[]{:S(2)}) collective-permute-start(bf16[2,500,128]{2,1,0:T(8,128)(2,1)S(1)} %slice.65), channel_id=1, source_target_pairs={{0,224},{16,240},{32,0},{48,16},{64,32},{80,48},{96,64},{112,80},{... | collective-permute-start | bytes 768008 | tf_op jit(solution)/shard_map/ppermute | solution.py:27
  172.1 44.5 %collective-permute-start.22 = (bf16[4,500,256]{2,0,1:T(4,128)(2,1)}, bf16[4,500,256]{2,0,1:T(4,128)(2,1)}, u32[]{:S(2)}, u32[]{:S(2)}) collective-permute-start(bf16[4,500,256]{2,0,1:T(4,128)(2,1)} %copy.17), channel_id=1, source_target_pairs={{0,16},{16,0},{32,48},{48,32},{64,80},{80,64},{96,112},{112,96},{1... | collective-permute-start | bytes 3072008 | tf_op jit(solution)/shard_map/ppermute | solution.py:27
  177.6 47.3 %collective-permute-start.16 = (bf16[4,500,256]{2,0,1:T(4,128)(2,1)}, bf16[4,500,256]{2,0,1:T(4,128)(2,1)}, u32[]{:S(2)}, u32[]{:S(2)}) collective-permute-start(bf16[4,500,256]{2,0,1:T(4,128)(2,1)} %copy.11), channel_id=1, source_target_pairs={{0,16},{16,0},{32,48},{48,32},{64,80},{80,64},{96,112},{112,96},{1... | collective-permute-start | bytes 3072008 | tf_op jit(solution)/shard_map/ppermute | solution.py:27
  183.5 11.8 %copy-start.5 = (bf16[4,500,256]{2,1,0:T(8,128)(2,1)S(1)}, bf16[4,500,256]{2,1,0:T(8,128)(2,1)}, u32[]{:S(2)}) copy-start(bf16[4,500,256]{2,1,0:T(8,128)(2,1)} %copy.16.b_ref) | copy-start | bytes 3072004
  195.3 6.6 %copy-start.3 = (bf16[4,500,256]{2,1,0:T(8,128)(2,1)S(1)}, bf16[4,500,256]{2,1,0:T(8,128)(2,1)}, u32[]{:S(2)}) copy-start(bf16[4,500,256]{2,1,0:T(8,128)(2,1)} %copy-done.2) | copy-start | bytes 3072004
  195.3 6.6 %copy-start.4 = (bf16[4,500,256]{2,1,0:T(8,128)(2,1)S(1)}, bf16[4,500,256]{2,1,0:T(8,128)(2,1)}, u32[]{:S(2)}) copy-start(bf16[4,500,256]{2,1,0:T(8,128)(2,1)} %copy.14.b_ref) | copy-start | bytes 3072004
  200.7 5.8 %copy-start.6 = (f32[4,96,256]{2,1,0:T(8,128)}, f32[4,96,256]{2,1,0:T(8,128)S(1)}, u32[]{:S(2)}) copy-start(f32[4,96,256]{2,1,0:T(8,128)S(1)} %get-tuple-element.17) | copy-start | bytes 1179652
  200.7 9.0 %collective-permute-start.21 = (bf16[4,96,256]{2,1,0:T(8,128)(2,1)}, bf16[4,96,256]{2,1,0:T(8,128)(2,1)S(1)}, u32[]{:S(2)}, u32[]{:S(2)}) collective-permute-start(bf16[4,96,256]{2,1,0:T(8,128)(2,1)} %get-tuple-element.18), channel_id=1, source_target_pairs={{0,1},{16,17},{32,33},{48,49},{64,65},{80,81},{96,97},{112,113},{1... | collective-permute-start | bytes 589832 | tf_op jit(solution)/shard_map/ppermute | solution.py:27
  206.5 8.8 %collective-permute-start.19 = (bf16[4,96,256]{2,1,0:T(8,128)(2,1)S(1)}, bf16[4,96,256]{2,1,0:T(8,128)(2,1)S(1)}, u32[]{:S(2)}, u32[]{:S(2)}) collective-permute-start(bf16[4,96,256]{2,1,0:T(8,128)(2,1)S(1)} %get-tuple-element.16), channel_id=1, source_target_pairs={{0,1},{16,17},{32,33},{48,49},{64,65},{80,81},{96,97},{112,113},{1... | collective-permute-start | bytes 589832 | tf_op jit(solution)/shard_map/ppermute | solution.py:27
  222.5 9.7 %collective-permute-start.23 = (bf16[4,96,256]{2,1,0:T(8,128)(2,1)S(1)}, bf16[4,96,256]{2,1,0:T(8,128)(2,1)S(1)}, u32[]{:S(2)}, u32[]{:S(2)}) collective-permute-start(bf16[4,96,256]{2,1,0:T(8,128)(2,1)S(1)} %get-tuple-element.20), channel_id=1, source_target_pairs={{0,1},{16,17},{32,33},{48,49},{64,65},{80,81},{96,97},{112,113},{1... | collective-permute-start | bytes 589832 | tf_op jit(solution)/shard_map/ppermute | solution.py:27
  230.9 7.5 %collective-permute-start.17 = (bf16[4,96,256]{2,1,0:T(8,128)(2,1)S(1)}, bf16[4,96,256]{2,1,0:T(8,128)(2,1)S(1)}, u32[]{:S(2)}, u32[]{:S(2)}) collective-permute-start(bf16[4,96,256]{2,1,0:T(8,128)(2,1)S(1)} %get-tuple-element.14), channel_id=1, source_target_pairs={{0,1},{16,17},{32,33},{48,49},{64,65},{80,81},{96,97},{112,113},{1... | collective-permute-start | bytes 589832 | tf_op jit(solution)/shard_map/ppermute | solution.py:27
  239.4 4.0 %copy-start.1 = (bf16[96,8,128]{2,1,0:T(8,128)(2,1)S(1)}, bf16[96,8,128]{2,1,0:T(8,128)(2,1)}, u32[]{:S(2)}) copy-start(bf16[96,8,128]{2,1,0:T(8,128)(2,1)} %param.3) | copy-start | bytes 589828
  (1 other events, 0.9 us)

commit v2 on v0

v2 whole, which is shorter than its diff:
```python
import jax
import jax.numpy as jnp
from jax import lax
from jax.experimental import pallas as pl
from jax.experimental.pallas import tpu as pltpu
from jax.sharding import Mesh, PartitionSpec as P

NC, NG = 8, 500
AXES = ("z", "core", "y", "x_lo", "pair")
SIZES = (8, 2, 4, 2, 2)
MIB = 1 << 20
F32, BF16 = jnp.float32, jnp.bfloat16
CHUNKS = ((0, 2), (2, 2))


def flat(x, y, z, c):
    x, y, z, c = x % 4, y % 4, z % 8, c % 2
    return ((z * 2 + c) * 8 + (y * 2 + x % 2)) * 2 + x // 2


def send(value, dx=0, dy=0, dz=0, dc=0):
    pairs = [
        (flat(x, y, z, c), flat(x + dx, y + dy, z + dz, c + dc))
        for x in range(4)
        for y in range(4)
        for z in range(8)
        for c in range(2)
    ]
    return lax.ppermute(value, AXES, pairs)


def exchange(value, axes):
    return lax.all_to_all(value, axes, 0, 0, tiled=True)


def params(mib=48):
    return pltpu.CompilerParams(vmem_limit_bytes=mib * MIB)


def cost(flops, nbytes):
    return pl.CostEstimate(flops=flops, bytes_accessed=nbytes, transcendentals=0)


def extract_kernel(lo_ref, hi_ref, sel_ref, *rest):
    v_refs, w_ref, f_ref = rest[:-2], rest[-2], rest[-1]
    first = 4 * lax.axis_index("pair")
    g = lax.broadcasted_iota(jnp.int32, (16, 64, 128), 0) + (256 + 16 * pl.program_id(0))
    halves = (lo_ref[...], jnp.where(g < NG, hi_ref[...], 0))
    for h, x in enumerate(halves):
        f_ref[h] = x.astype(F32).reshape(16 * 64, 128)
    for h in range(2):
        for j in range(8):
            for (start, count), v_ref in zip(CHUNKS, v_refs):
                for b in range(count):
                    row = f_ref[h, pl.ds(8 * j + first + start + b, 16, stride=64), :]
                    v_ref[j, b, h] = row.astype(BF16)
    lhs = jnp.concatenate(
        [jnp.concatenate([halves[0][i], halves[1][i]], axis=0) for i in range(16)], axis=1
    )
    picked = jnp.dot(lhs, sel_ref[...], preferred_element_type=F32)
    w_ref[...] = jnp.transpose(picked).astype(BF16).reshape(NC, 16, 128)


def extract(vertex):
    by_g = jnp.transpose(vertex, (2, 0, 1))
    i, d = jnp.arange(2048) // 128, jnp.arange(2048) % 128
    c2, i2 = jnp.arange(128) // 16, jnp.arange(128) % 16
    sel = ((i[:, None] == i2[None]) & (d[:, None] == c2[None])).astype(BF16)
    outs = pl.pallas_call(
        extract_kernel,
        grid=(16,),
        in_specs=[
            pl.BlockSpec((16, 64, 128), lambda u: (u, 0, 0)),
            pl.BlockSpec((16, 64, 128), lambda u: (16 + u, 0, 0)),
            pl.BlockSpec((2048, 128), lambda u: (0, 0)),
        ],
        out_specs=[pl.BlockSpec((8, n, 2, 16, 128), lambda u: (0, 0, 0, u, 0)) for _, n in CHUNKS]
        + [pl.BlockSpec((NC, 16, 128), lambda u: (0, u, 0))],
        out_shape=[jax.ShapeDtypeStruct((8, n, 2, 256, 128), BF16) for _, n in CHUNKS]
        + [jax.ShapeDtypeStruct((NC, 256, 128), BF16)],
        scratch_shapes=[pltpu.VMEM((2, 16 * 64, 128), F32)],
        compiler_params=params(),
        cost_estimate=cost(2 * 2048 * 2048 * 128, 14 * MIB),
    )(by_g, by_g, sel)
    return outs[:-1], outs[-1]


def amps_kernel(mine_ref, other_ref, t_ref):
    core, pair = lax.axis_index("core"), lax.axis_index("pair")
    for src, own in ((mine_ref, core), (other_ref, 1 - core)):
        for x in range(4):
            for y in range(4):
                j, k = y * 2 + x // 2, x % 2
                for c in range(4):
                    t_ref[own * 4 + c, lax.rem(pair + k, 2), :, j * 128 : (j + 1) * 128] = src[x, y, c]


def gather_amps(mine, other):
    return pl.pallas_call(
        amps_kernel,
        out_shape=jax.ShapeDtypeStruct((NC, 2, 96, 1024), BF16),
        compiler_params=params(),
        cost_estimate=cost(0, 7 * MIB),
    )(mine, other)


def inner_kernel(t_ref, v_ref, out_ref):
    v = jnp.concatenate([v_ref[j, 0].reshape(512, 128) for j in range(8)], axis=-1)
    t = t_ref[...].reshape(NC * 192, 1024)
    prod = lax.dot_general(t, v, (((1,), (1,)), ((), ())), preferred_element_type=F32)
    out_ref[...] = prod.astype(BF16).reshape(NC, 1, 192, 512)


def inner_terms(t, v):
    nb = v.shape[1]
    return pl.pallas_call(
        inner_kernel,
        grid=(nb,),
        in_specs=[
            pl.BlockSpec((NC, 2, 96, 1024), lambda b: (0, 0, 0, 0)),
            pl.BlockSpec((8, 1, 2, 256, 128), lambda b: (0, b, 0, 0, 0)),
        ],
        out_specs=pl.BlockSpec((NC, 1, 192, 512), lambda b: (0, b, 0, 0)),
        out_shape=jax.ShapeDtypeStruct((NC, nb, 192, 512), BF16),
        compiler_params=params(),
        cost_estimate=cost(2 * nb * 1536 * 1024 * 512, 8 * MIB),
    )(t, v)


def ladder_kernel(*refs):
    s_refs, (mine0, mine1, far0, far1, own_ref, give_ref) = refs[:-6], refs[-6:]
    core = lax.axis_index("core")
    low = lax.broadcasted_iota(jnp.int32, (256, 128), 1) < 64
    totals = [None] * len(s_refs)
    for c in range(NC):
        weights = []
        for mine_ref, far_ref in ((mine0, far0), (mine1, far1)):
            mine, far = mine_ref[c].astype(F32), far_ref[c].astype(F32)
            one = jnp.where(core == 0, mine, far)
            two = jnp.where(core == 0, far, mine)
            lo = jnp.where(low, one, pltpu.roll(two, 64, 1))
            hi = jnp.where(low, pltpu.roll(one, 64, 1), two)
            weights.append(jnp.concatenate([lo, hi], axis=0).astype(BF16))
        weight = jnp.concatenate(weights, axis=1)
        for n, s_ref in enumerate(s_refs):
            lhs = s_ref[c].reshape(-1, 512)
            p = jnp.dot(lhs, weight, preferred_element_type=F32)
            totals[n] = p if totals[n] is None else totals[n] + p
    row = 0
    for total in totals:
        total = total.reshape(-1, 2, 96, 256)
        n = total.shape[0]
        own_ref[row : row + n] = total[:, 0]
        give_ref[row : row + n] = total[:, 1].astype(BF16)
        row += n


def ladder_part(inner, mine, far):
    return pl.pallas_call(
        ladder_kernel,
        out_shape=(
            jax.ShapeDtypeStruct((4, 96, 256), F32),
            jax.ShapeDtypeStruct((4, 96, 256), BF16),
        ),
        compiler_params=params(),
        cost_estimate=cost(2 * 768 * 4096 * 256, 10 * MIB),
    )(*inner, *mine, *far)


def assemble_kernel(*refs):
    own_refs, got_refs, out_ref = refs[:4], refs[4:8], refs[8]
    z, pair = lax.axis_index("z"), lax.axis_index("pair")

    def place(mine, theirs):
        for i, (own_ref, got_ref) in enumerate(zip(own_refs, got_refs)):
            for h, shift in enumerate(SHIFTS[i]):
                start = pl.multiple_of(lax.rem(z + 8 + shift, 8) * 128, 128)
                for b in range(4):
                    lanes = slice(h * 128, (h + 1) * 128)
                    out_ref[:, mine + b, pl.ds(start, 128)] = own_ref[b, :, lanes]
                    out_ref[:, theirs + b, pl.ds(start, 128)] = got_ref[b, :, lanes].astype(F32)

    @pl.when(pair == 0)
    def _():
        place(0, 4)

    @pl.when(pair == 1)
    def _():
        place(4, 0)


SHIFTS = ((-1, 1), (-2, 2), (-3, 3), (0, 4))


def assemble(own, got):
    return pl.pallas_call(
        assemble_kernel,
        grid=(6,),
        in_specs=[pl.BlockSpec((4, 16, 256), lambda p: (0, p, 0))] * 8,
        out_specs=pl.BlockSpec((16, 8, 1024), lambda p: (p, 0, 0)),
        out_shape=jax.ShapeDtypeStruct((96, 8, 1024), F32),
        compiler_params=params(),
        cost_estimate=cost(0, 6 * MIB),
    )(*own, *got)


def per_device(vertex, amps):
    core, pair = lax.axis_index("core"), lax.axis_index("pair")
    chunks, w = extract(vertex)

    piece = exchange(w.reshape(16, 128, 128), ("y", "x_lo", "pair"))
    piece = lax.dynamic_slice_in_dim(piece, pair, 1, 0)
    w = exchange(jnp.broadcast_to(piece, (16, 128, 128)), ("y", "x_lo", "pair"))
    w = w.reshape(NC, 256, 128)

    t = jnp.transpose(amps, (1, 0, 2))
    t = lax.dynamic_slice_in_dim(t, core * 4, 4, 0)
    t = exchange(jnp.broadcast_to(t[None], (4, 4, 96, 128)), "y")
    t = exchange(jnp.broadcast_to(t[None], (4, 4, 4, 96, 128)).reshape(4, 4, 4, 96, 128), ("x_lo", "pair"))
    t = gather_amps(t, send(t, dc=1))

    inner = [inner_terms(t, exchange(v, ("y", "x_lo"))) for v in chunks]

    ups, downs = [w], [w]
    for _ in range(3):
        ups.append(send(ups[-1], dz=1))
        downs.append(send(downs[-1], dz=-1))
    opposite = jnp.concatenate([send(ups[-1][:4], dz=1), send(downs[-1][4:], dz=-1)], 0)

    own, got = [], []
    for blocks in [(ups[i], downs[i]) for i in (1, 2, 3)] + [(w, opposite)]:
        far = [send(block, dc=1) for block in blocks]
        mine, give = ladder_part(inner, blocks, far)
        own.append(mine)
        got.append(send(give, dx=2))
    return assemble(own, got)


def solution(mesh):
    fine = Mesh(mesh.devices.reshape(SIZES), AXES)
    return jax.shard_map(
        per_device,
        mesh=fine,
        in_specs=(P(("z", "core"), ("y", "x_lo"), None), P("pair", None, ("y", "x_lo"))),
        out_specs=P("pair", ("z", "core", "y", "x_lo"), None),
        check_vma=False,
    )
```

time: 553 us -> 209 us (0.38); the launches traced: 544 us -> 207 us
  waiting for transfers between devices: 474 us -> 52.1 us
  Pallas kernels: 0 us -> 51.9 us
  starting transfers between devices: 7.18 us -> 56.3 us
  blocking collectives: 0 us -> 33.9 us
  matrix products: 24 us -> 0 us
  local copies, waits for them, and re-layouts: 26 us -> 11.4 us
  between operations: 13.4 us -> 0.2 us
    all_gather x2 -> x0, waiting for transfers between devices: 356 us -> none  [the longest x1 356 us: per_device(): lax.all_gather(vertex_rows[:, :NC, :], ('vrow', 'vcol'), axis=0, tiled=True)]
    all_to_all x1 -> x4, waiting for transfers between devices: 117 us -> 16.4 us  [exchange(): return lax.all_to_all(value, axes, 0, 0, tiled=True)]
    pallas_call x0 -> x9, Pallas kernels: none -> 51.9 us  [the longest x4 17.1 us: ladder_part(): pl.pallas_call(ladder_kernel, out_shape=(jax.ShapeDtypeStruct((4, 96, 256...]
    ppermute x0 -> x21, waiting for transfers between devices: none -> 35.8 us  [send(): return lax.ppermute(value, AXES, pairs)]
    all_to_all x0 -> x2, blocking collectives: none -> 33.9 us  [exchange(): return lax.all_to_all(value, axes, 0, 0, tiled=True)]
    ppermute x0 -> x21, starting transfers between devices: none -> 28.4 us  [send(): return lax.ppermute(value, AXES, pairs)]
    dot_general x2 -> x0, matrix products: 24 us -> none  [the longest x1 12.6 us: per_device(): lax.dot_general(inner_terms, lax.all_gather(vertex_rows[:, :NC, :], ('vro...]
    all_to_all x1 -> x4, starting transfers between devices: 6.96 us -> 27.9 us  [exchange(): return lax.all_to_all(value, axes, 0, 0, tiled=True)]
  transfers between devices with their start and end apart: 3 -> 25, of which waited for: 2 -> 9; matrix products, arithmetic and copies ran while one was open for 5% -> 2% of each run, Pallas kernels for 0% -> 15%
where the time goes in v2:
time: 209 us; the launch traced here: 207 us
  starting transfers between devices  56.3 us (27%)
  waiting for transfers between devices  52.1 us (25%)
  Pallas kernels  51.9 us (25%)
  blocking collectives  33.9 us (16%)
  local copies, waits for them, and re-layouts  11.4 us (5%)
    ppermute x21, waiting for transfers between devices, send(): return lax.ppermute(value, AXES, pairs)  35.8 us
    all_to_all x2, blocking collectives, exchange(): return lax.all_to_all(value, axes, 0, 0, tiled=True)  33.9 us
    ppermute x21, starting transfers between devices, send(): return lax.ppermute(value, AXES, pairs)  28.4 us
    all_to_all x4, starting transfers between devices, exchange(): return lax.all_to_all(value, axes, 0, 0, tiled=True)  27.9 us
    pallas_call x4, Pallas kernels, ladder_part(): pl.pallas_call(ladder_kernel, out_shape=(jax.ShapeDtypeStruct((4, 96, 256...  17.1 us
    all_to_all x4, waiting for transfers between devices, exchange(): return lax.all_to_all(value, axes, 0, 0, tiled=True)  16.4 us
    pallas_call x1, Pallas kernels, extract(): pl.pallas_call(extract_kernel, grid=(16,), in_specs=[pl.BlockSpec((16, 64...  15.7 us
    pallas_call x2, Pallas kernels, inner_terms(): pl.pallas_call(inner_kernel, grid=(nb,), in_specs=[pl.BlockSpec((NC, 2, 9...  12.3 us
  transfers between devices with their start and end apart: 25, of which 9 were waited for; matrix products, arithmetic and copies ran while one was open for 2% of the time, Pallas kernels for 15%

profile of v2, /device:TPU:18, one launch (start us, length us, event | category | flops | bytes accessed | tf_op | source)
XLA Modules:
  0.0 207.2 jit_solution(6270444504186737955)
XLA Ops:
  1.3 15.7 %shard_map.29 = (bf16[8,2,2,256,128]{4,3,2,1,0:T(8,128)(2,1)S(1)}, bf16[8,2,2,256,128]{4,3,2,1,0:T(8,128)(2,1)S(1)}, bf16[8,256,128]{2,1,0:T(8,128)(2,1)}) custom-call(bf16[500,64,128]{2,1,0:T(8,128)(2,1)} %bitcast.7, bf16[500,64,128]{2,1,0:T(8,128)(2,1)} %bitcast.8, bf16[2048,128]{1,0:T(8,128)(2,1)S(1)} %and_convert_fusion.sel_ref), custom_call_target="tpu_custom_call" | custom-call | flops 1073741824 | bytes 14680064 | tf_op jit(solution)/shard_map/pallas_call | solution.py:69
  17.0 1.3 copy-done.2
  19.7 7.3 %all-to-all-start.4 = ((bf16[16,128,128]{2,1,0:T(8,128)(2,1)}), bf16[16,128,128]{2,1,0:T(8,128)(2,1)S(1)}, u32[]{:S(2)}, u32[]{:S(2)}) async-start(bf16[16,128,128]{2,1,0:T(8,128)(2,1)} %bitcast.2), calls=%async_computation.4 | async-start | bytes 1048576 | tf_op jit(solution)/shard_map/all_to_all | solution.py:33
  27.1 7.8 %all-to-all-done.4 = bf16[16,128,128]{2,1,0:T(8,128)(2,1)S(1)} async-done(((bf16[16,128,128]{2,1,0:T(8,128)(2,1)}), bf16[16,128,128]{2,1,0:T(8,128)(2,1)S(1)}, u32[]{:S(2)}, u32[]{:S(2)}) %all-to-all-start.4) | async-done | bytes 524320 | tf_op jit(solution)/shard_map/all_to_all | solution.py:33
  35.7 5.4 %all-to-all-start = ((bf16[4,4,96,128]{3,2,1,0:T(8,128)(2,1)}), bf16[4,4,96,128]{3,2,1,0:T(8,128)(2,1)S(1)}, u32[]{:S(2)}, u32[]{:S(2)}) async-start(bf16[4,4,96,128]{3,2,1,0:T(8,128)(2,1)} %broadcast_in_dim.8), calls=%async_computation | async-start | bytes 786432 | tf_op jit(solution)/shard_map/all_to_all | solution.py:33
  41.1 4.4 %all-to-all-done = bf16[4,4,96,128]{3,2,1,0:T(8,128)(2,1)S(1)} async-done(((bf16[4,4,96,128]{3,2,1,0:T(8,128)(2,1)}), bf16[4,4,96,128]{3,2,1,0:T(8,128)(2,1)S(1)}, u32[]{:S(2)}, u32[]{:S(2)}) %all-to-all-start) | async-done | bytes 393248 | tf_op jit(solution)/shard_map/all_to_all | solution.py:33
  45.6 14.1 %all_to_all.30 = bf16[16,128,128]{2,1,0:T(8,128)(2,1)} all-to-all(bf16[16,128,128]{2,1,0:T(8,128)(2,1)S(1)} %broadcast_in_dim.11), channel_id=1, replica_groups=mesh['z'=8,'core'=2,'y'=4,'x_lo'=2,'pair'=2] {'y','x_lo','pair'}, dimensions={0} | all-to-all | bytes 1048576 | tf_op jit(solution)/shard_map/all_to_all | solution.py:33
  60.1 19.8 %all_to_all.31.mine_ref = bf16[4,4,4,96,128]{4,3,2,1,0:T(8,128)(2,1)S(1)} all-to-all(bf16[4,4,4,96,128]{4,3,2,1,0:T(8,128)(2,1)S(1)} %broadcast_in_dim.9), channel_id=1, replica_groups=mesh['z'=8,'core'=2,'y'=4,'x_lo'=2,'pair'=2] {'x_lo','pair'}, dimensions={0} | all-to-all | bytes 3145728 | tf_op jit(solution)/shard_map/all_to_all | solution.py:33
  79.9 7.3 %all-to-all-start.2 = ((bf16[8,2,2,256,128]{4,3,2,1,0:T(8,128)(2,1)}), bf16[8,2,2,256,128]{4,3,2,1,0:T(8,128)(2,1)}, u32[]{:S(2)}, u32[]{:S(2)}) async-start(bf16[8,2,2,256,128]{4,3,2,1,0:T(8,128)(2,1)} %copy-done.3), calls=%async_computation.2 | async-start | bytes 4194304 | tf_op jit(solution)/shard_map/all_to_all | solution.py:33
  87.2 1.9 collective-permute-start.1
  89.1 3.9 %collective-permute-start.2 = (bf16[8,256,128]{2,1,0:T(8,128)(2,1)}, bf16[8,256,128]{2,1,0:T(8,128)(2,1)}, u32[]{:S(2)}, u32[]{:S(2)}) collective-permute-start(bf16[8,256,128]{2,1,0:T(8,128)(2,1)} %bitcast.4.refs_2_), channel_id=1, source_target_pairs={{0,224},{16,240},{32,0},{48,16},{64,32},{80,48},{96,64},{112,80},{... | collective-permute-start | bytes 1572872 | tf_op jit(solution)/shard_map/ppermute | solution.py:29
  93.0 9.1 %collective-permute-done.1.refs_2_ = bf16[8,256,128]{2,1,0:T(8,128)(2,1)} collective-permute-done((bf16[8,256,128]{2,1,0:T(8,128)(2,1)}, bf16[8,256,128]{2,1,0:T(8,128)(2,1)}, u32[]{:S(2)}, u32[]{:S(2)}) %collective-permute-start.1) | collective-permute-done | bytes 524320 | tf_op jit(solution)/shard_map/ppermute | solution.py:29
  102.2 4.1 %all-to-all-done.2.v_ref = bf16[8,2,2,256,128]{4,3,2,1,0:T(8,128)(2,1)} async-done(((bf16[8,2,2,256,128]{4,3,2,1,0:T(8,128)(2,1)}), bf16[8,2,2,256,128]{4,3,2,1,0:T(8,128)(2,1)}, u32[]{:S(2)}, u32[]{:S(2)}) %all-to-all-start.2) | async-done | bytes 2097184 | tf_op jit(solution)/shard_map/all_to_all | solution.py:33
  106.3 7.8 %all-to-all-start.3 = ((bf16[8,2,2,256,128]{4,3,2,1,0:T(8,128)(2,1)}), bf16[8,2,2,256,128]{4,3,2,1,0:T(8,128)(2,1)}, u32[]{:S(2)}, u32[]{:S(2)}) async-start(bf16[8,2,2,256,128]{4,3,2,1,0:T(8,128)(2,1)} %copy-done.2), calls=%async_computation.3 | async-start | bytes 4194304 | tf_op jit(solution)/shard_map/all_to_all | solution.py:33
  114.2 5.9 %collective-permute-start.6 = (bf16[8,256,128]{2,1,0:T(8,128)(2,1)}, bf16[8,256,128]{2,1,0:T(8,128)(2,1)}, u32[]{:S(2)}, u32[]{:S(2)}) collective-permute-start(bf16[8,256,128]{2,1,0:T(8,128)(2,1)} %collective-permute-done.2.refs_3_), channel_id=1, source_target_pairs={{0,224},{16,240},{32,0},{48,16},{64,32},{80,48},{96,64},{112,80},{... | collective-permute-start | bytes 1572872 | tf_op jit(solution)/shard_map/ppermute | solution.py:29
  120.0 9.9 %collective-permute-done.6.refs_3_ = bf16[8,256,128]{2,1,0:T(8,128)(2,1)} collective-permute-done((bf16[8,256,128]{2,1,0:T(8,128)(2,1)}, bf16[8,256,128]{2,1,0:T(8,128)(2,1)}, u32[]{:S(2)}, u32[]{:S(2)}) %collective-permute-start.6) | collective-permute-done | bytes 524320 | tf_op jit(solution)/shard_map/ppermute | solution.py:29
  129.9 3.7 %collective-permute-start.10 = (bf16[8,256,128]{2,1,0:T(8,128)(2,1)}, bf16[8,256,128]{2,1,0:T(8,128)(2,1)}, u32[]{:S(2)}, u32[]{:S(2)}) collective-permute-start(bf16[8,256,128]{2,1,0:T(8,128)(2,1)} %collective-permute-done.6.refs_3_), channel_id=1, source_target_pairs={{0,224},{16,240},{32,0},{48,16},{64,32},{80,48},{96,64},{112,80},{... | collective-permute-start | bytes 1572872 | tf_op jit(solution)/shard_map/ppermute | solution.py:29
  134.7 8.8 %collective-permute-done.10.refs_3_ = bf16[8,256,128]{2,1,0:T(8,128)(2,1)} collective-permute-done((bf16[8,256,128]{2,1,0:T(8,128)(2,1)}, bf16[8,256,128]{2,1,0:T(8,128)(2,1)}, u32[]{:S(2)}, u32[]{:S(2)}) %collective-permute-start.10) | collective-permute-done | bytes 524320 | tf_op jit(solution)/shard_map/ppermute | solution.py:29
  144.4 3.8 %collective-permute-start.14 = (bf16[4,256,128]{2,1,0:T(8,128)(2,1)S(1)}, bf16[4,256,128]{2,1,0:T(8,128)(2,1)S(1)}, u32[]{:S(2)}, u32[]{:S(2)}) collective-permute-start(bf16[4,256,128]{2,1,0:T(8,128)(2,1)S(1)} %slice.9), channel_id=1, source_target_pairs={{0,224},{16,240},{32,0},{48,16},{64,32},{80,48},{96,64},{112,80},{... | collective-permute-start | bytes 786440 | tf_op jit(solution)/shard_map/ppermute | solution.py:29
  149.4 2.6 %collective-permute-done.14 = bf16[4,256,128]{2,1,0:T(8,128)(2,1)S(1)} collective-permute-done((bf16[4,256,128]{2,1,0:T(8,128)(2,1)S(1)}, bf16[4,256,128]{2,1,0:T(8,128)(2,1)S(1)}, u32[]{:S(2)}, u32[]{:S(2)}) %collective-permute-start.14) | collective-permute-done | bytes 262176 | tf_op jit(solution)/shard_map/ppermute | solution.py:29
  153.3 2.6 %shard_map.28.t_ref = bf16[8,2,96,1024]{3,2,1,0:T(8,128)(2,1)} custom-call(bf16[4,4,4,96,128]{4,3,2,1,0:T(8,128)(2,1)S(1)} %all_to_all.31.mine_ref, bf16[4,4,4,96,128]{4,3,2,1,0:T(8,128)(2,1)S(1)} %collective-permute-done.other_ref), custom_call_target="tpu_custom_call" | custom-call | bytes 7340032 | tf_op jit(solution)/shard_map/pallas_call | solution.py:99
  155.9 6.1 %shard_map.30.refs_0_ = bf16[8,2,192,512]{3,2,1,0:T(8,128)(2,1)S(1)} custom-call(bf16[8,2,96,1024]{3,2,1,0:T(8,128)(2,1)} %shard_map.28.t_ref, bf16[8,2,2,256,128]{4,3,2,1,0:T(8,128)(2,1)} %all-to-all-done.2.v_ref), custom_call_target="tpu_custom_call" | custom-call | flops 3221225472 | bytes 8388608 | tf_op jit(solution)/shard_map/pallas_call | solution.py:116
  164.9 6.2 %shard_map.31.refs_1_ = bf16[8,2,192,512]{3,2,1,0:T(8,128)(2,1)S(1)} custom-call(bf16[8,2,96,1024]{3,2,1,0:T(8,128)(2,1)} %shard_map.28.t_ref, bf16[8,2,2,256,128]{4,3,2,1,0:T(8,128)(2,1)} %all-to-all-done.3.v_ref), custom_call_target="tpu_custom_call" | custom-call | flops 3221225472 | bytes 8388608 | tf_op jit(solution)/shard_map/pallas_call | solution.py:116
  171.2 1.7 copy-done.1
  172.8 4.1 %shard_map.32 = (f32[4,96,256]{2,1,0:T(8,128)S(1)}, bf16[4,96,256]{2,1,0:T(8,128)(2,1)S(1)}) custom-call(bf16[8,2,192,512]{3,2,1,0:T(8,128)(2,1)S(1)} %shard_map.30.refs_0_, bf16[8,2,192,512]{3,2,1,0:T(8,128)(2,1)} %copy-done.1, bf16[8,256,128]{2,1,0:T(8,128)(2,1)} %collective-permute-done.1.refs_2_, bf16[8,256,128]{2,1,0:T(8,128)(2,1)} %collective-permute-done.2.refs_3_, ...), custom_call_target="tpu_custom_call" | custom-call | flops 1610612736 | bytes 10485760 | tf_op jit(solution)/shard_map/pallas_call | solution.py:159
  177.9 4.2 %shard_map.33 = (f32[4,96,256]{2,1,0:T(8,128)S(1)}, bf16[4,96,256]{2,1,0:T(8,128)(2,1)S(1)}) custom-call(bf16[8,2,192,512]{3,2,1,0:T(8,128)(2,1)S(1)} %shard_map.30.refs_0_, bf16[8,2,192,512]{3,2,1,0:T(8,128)(2,1)} %copy-done.1, bf16[8,256,128]{2,1,0:T(8,128)(2,1)} %collective-permute-done.5.refs_2_, bf16[8,256,128]{2,1,0:T(8,128)(2,1)} %collective-permute-done.6.refs_3_, ...), custom_call_target="tpu_custom_call" | custom-call | flops 1610612736 | bytes 10485760 | tf_op jit(solution)/shard_map/pallas_call | solution.py:159
  182.1 2.8 %collective-permute-start.18 = (bf16[4,96,256]{2,1,0:T(8,128)(2,1)S(1)}, bf16[4,96,256]{2,1,0:T(8,128)(2,1)S(1)}, u32[]{:S(2)}, u32[]{:S(2)}) collective-permute-start(bf16[4,96,256]{2,1,0:T(8,128)(2,1)S(1)} %get-tuple-element.24), channel_id=1, source_target_pairs={{0,1},{16,17},{32,33},{48,49},{64,65},{80,81},{96,97},{112,113},{1... | collective-permute-start | bytes 589832 | tf_op jit(solution)/shard_map/ppermute | solution.py:29
  184.9 4.4 %shard_map.34 = (f32[4,96,256]{2,1,0:T(8,128)S(1)}, bf16[4,96,256]{2,1,0:T(8,128)(2,1)S(1)}) custom-call(bf16[8,2,192,512]{3,2,1,0:T(8,128)(2,1)S(1)} %shard_map.30.refs_0_, bf16[8,2,192,512]{3,2,1,0:T(8,128)(2,1)} %copy-done.1, bf16[8,256,128]{2,1,0:T(8,128)(2,1)} %collective-permute-done.9.refs_2_, bf16[8,256,128]{2,1,0:T(8,128)(2,1)} %collective-permute-done.10.refs_3_, ...), custom_call_target="tpu_custom_call" | custom-call | flops 1610612736 | bytes 10485760 | tf_op jit(solution)/shard_map/pallas_call | solution.py:159
  190.4 4.4 %shard_map.35 = (f32[4,96,256]{2,1,0:T(8,128)S(1)}, bf16[4,96,256]{2,1,0:T(8,128)(2,1)S(1)}) custom-call(bf16[8,2,192,512]{3,2,1,0:T(8,128)(2,1)S(1)} %shard_map.30.refs_0_, bf16[8,2,192,512]{3,2,1,0:T(8,128)(2,1)} %copy-done.1, bf16[8,256,128]{2,1,0:T(8,128)(2,1)} %bitcast.4.refs_2_, bf16[8,256,128]{2,1,0:T(8,128)(2,1)} %constant_dynamic-update-slice_fusion.refs_3_, ...), custom_call_target="tpu_custom_call" | custom-call | flops 1610612736 | bytes 10485760 | tf_op jit(solution)/shard_map/pallas_call | solution.py:159
  194.8 2.8 %collective-permute-start.20 = (bf16[4,96,256]{2,1,0:T(8,128)(2,1)S(1)}, bf16[4,96,256]{2,1,0:T(8,128)(2,1)S(1)}, u32[]{:S(2)}, u32[]{:S(2)}) collective-permute-start(bf16[4,96,256]{2,1,0:T(8,128)(2,1)S(1)} %get-tuple-element.26), channel_id=1, source_target_pairs={{0,1},{16,17},{32,33},{48,49},{64,65},{80,81},{96,97},{112,113},{1... | collective-permute-start | bytes 589832 | tf_op jit(solution)/shard_map/ppermute | solution.py:29
  197.8 5.1 %collective-permute-done.20.refs_7_ = bf16[4,96,256]{2,1,0:T(8,128)(2,1)S(1)} collective-permute-done((bf16[4,96,256]{2,1,0:T(8,128)(2,1)S(1)}, bf16[4,96,256]{2,1,0:T(8,128)(2,1)S(1)}, u32[]{:S(2)}, u32[]{:S(2)}) %collective-permute-start.20) | collective-permute-done | bytes 196640 | tf_op jit(solution)/shard_map/ppermute | solution.py:29
  202.9 4.3 %shard_map.36 = f32[96,8,1024]{2,1,0:T(8,128)} custom-call(f32[4,96,256]{2,1,0:T(8,128)S(1)} %get-tuple-element.19.refs_0_, f32[4,96,256]{2,1,0:T(8,128)S(1)} %get-tuple-element.20.refs_1_, f32[4,96,256]{2,1,0:T(8,128)S(1)} %get-tuple-element.21.refs_2_, f32[4,96,256]{2,1,0:T(8,128)S(1)} %get-tuple-element.22.refs_3_, ...), custom_call_target="tpu_custom_call" | custom-call | bytes 6291456 | tf_op jit(solution)/shard_map/pallas_call | solution.py:196
  (62 shorter events, 13.8 us)
Async XLA Ops:
  0.0 27.0 %copy-start = (bf16[96,8,128]{2,1,0:T(8,128)(2,1)S(1)}, bf16[96,8,128]{2,1,0:T(8,128)(2,1)}, u32[]{:S(2)}) copy-start(bf16[96,8,128]{2,1,0:T(8,128)(2,1)} %param.3) | copy-start | bytes 589828
  17.0 1.4 copy-start.2
  18.4 1.3 copy-start.3
  19.7 15.2 %all-to-all-start.4 = ((bf16[16,128,128]{2,1,0:T(8,128)(2,1)}), bf16[16,128,128]{2,1,0:T(8,128)(2,1)S(1)}, u32[]{:S(2)}, u32[]{:S(2)}) async-start(bf16[16,128,128]{2,1,0:T(8,128)(2,1)} %bitcast.2), calls=%async_computation.4 | async-start | bytes 1048576 | tf_op jit(solution)/shard_map/all_to_all | solution.py:33
  35.7 9.8 %all-to-all-start = ((bf16[4,4,96,128]{3,2,1,0:T(8,128)(2,1)}), bf16[4,4,96,128]{3,2,1,0:T(8,128)(2,1)S(1)}, u32[]{:S(2)}, u32[]{:S(2)}) async-start(bf16[4,4,96,128]{3,2,1,0:T(8,128)(2,1)} %broadcast_in_dim.8), calls=%async_computation | async-start | bytes 786432 | tf_op jit(solution)/shard_map/all_to_all | solution.py:33
  79.9 26.5 %all-to-all-start.2 = ((bf16[8,2,2,256,128]{4,3,2,1,0:T(8,128)(2,1)}), bf16[8,2,2,256,128]{4,3,2,1,0:T(8,128)(2,1)}, u32[]{:S(2)}, u32[]{:S(2)}) async-start(bf16[8,2,2,256,128]{4,3,2,1,0:T(8,128)(2,1)} %copy-done.3), calls=%async_computation.2 | async-start | bytes 4194304 | tf_op jit(solution)/shard_map/all_to_all | solution.py:33
  87.2 15.0 %collective-permute-start.1 = (bf16[8,256,128]{2,1,0:T(8,128)(2,1)}, bf16[8,256,128]{2,1,0:T(8,128)(2,1)}, u32[]{:S(2)}, u32[]{:S(2)}) collective-permute-start(bf16[8,256,128]{2,1,0:T(8,128)(2,1)} %bitcast.4.refs_2_), channel_id=1, source_target_pairs={{0,32},{16,48},{32,64},{48,80},{64,96},{80,112},{96,128},{112,144}... | collective-permute-start | bytes 1572872 | tf_op jit(solution)/shard_map/ppermute | solution.py:29
  89.1 25.1 %collective-permute-start.2 = (bf16[8,256,128]{2,1,0:T(8,128)(2,1)}, bf16[8,256,128]{2,1,0:T(8,128)(2,1)}, u32[]{:S(2)}, u32[]{:S(2)}) collective-permute-start(bf16[8,256,128]{2,1,0:T(8,128)(2,1)} %bitcast.4.refs_2_), channel_id=1, source_target_pairs={{0,224},{16,240},{32,0},{48,16},{64,32},{80,48},{96,64},{112,80},{... | collective-permute-start | bytes 1572872 | tf_op jit(solution)/shard_map/ppermute | solution.py:29
  93.0 59.8 %collective-permute-start = (bf16[4,4,4,96,128]{4,3,2,1,0:T(8,128)(2,1)S(1)}, bf16[4,4,4,96,128]{4,3,2,1,0:T(8,128)(2,1)S(1)}, u32[]{:S(2)}, u32[]{:S(2)}) collective-permute-start(bf16[4,4,4,96,128]{4,3,2,1,0:T(8,128)(2,1)S(1)} %all_to_all.31.mine_ref), channel_id=1, source_target_pairs={{0,16},{16,0},{32,48},{48,32},{64,80},{80,64},{96,112},{112,96},{1... | collective-permute-start | bytes 4718600 | tf_op jit(solution)/shard_map/ppermute | solution.py:29
  102.2 17.8 %collective-permute-start.5 = (bf16[8,256,128]{2,1,0:T(8,128)(2,1)}, bf16[8,256,128]{2,1,0:T(8,128)(2,1)}, u32[]{:S(2)}, u32[]{:S(2)}) collective-permute-start(bf16[8,256,128]{2,1,0:T(8,128)(2,1)} %collective-permute-done.1.refs_2_), channel_id=1, source_target_pairs={{0,32},{16,48},{32,64},{48,80},{64,96},{80,112},{96,128},{112,144}... | collective-permute-start | bytes 1572872 | tf_op jit(solution)/shard_map/ppermute | solution.py:29
  106.3 58.6 %all-to-all-start.3 = ((bf16[8,2,2,256,128]{4,3,2,1,0:T(8,128)(2,1)}), bf16[8,2,2,256,128]{4,3,2,1,0:T(8,128)(2,1)}, u32[]{:S(2)}, u32[]{:S(2)}) async-start(bf16[8,2,2,256,128]{4,3,2,1,0:T(8,128)(2,1)} %copy-done.2), calls=%async_computation.3 | async-start | bytes 4194304 | tf_op jit(solution)/shard_map/all_to_all | solution.py:33
  114.2 15.8 %collective-permute-start.6 = (bf16[8,256,128]{2,1,0:T(8,128)(2,1)}, bf16[8,256,128]{2,1,0:T(8,128)(2,1)}, u32[]{:S(2)}, u32[]{:S(2)}) collective-permute-start(bf16[8,256,128]{2,1,0:T(8,128)(2,1)} %collective-permute-done.2.refs_3_), channel_id=1, source_target_pairs={{0,224},{16,240},{32,0},{48,16},{64,32},{80,48},{96,64},{112,80},{... | collective-permute-start | bytes 1572872 | tf_op jit(solution)/shard_map/ppermute | solution.py:29
  120.0 13.6 %collective-permute-start.9 = (bf16[8,256,128]{2,1,0:T(8,128)(2,1)}, bf16[8,256,128]{2,1,0:T(8,128)(2,1)}, u32[]{:S(2)}, u32[]{:S(2)}) collective-permute-start(bf16[8,256,128]{2,1,0:T(8,128)(2,1)} %collective-permute-done.5.refs_2_), channel_id=1, source_target_pairs={{0,32},{16,48},{32,64},{48,80},{64,96},{80,112},{96,128},{112,144}... | collective-permute-start | bytes 1572872 | tf_op jit(solution)/shard_map/ppermute | solution.py:29
  129.9 13.5 %collective-permute-start.10 = (bf16[8,256,128]{2,1,0:T(8,128)(2,1)}, bf16[8,256,128]{2,1,0:T(8,128)(2,1)}, u32[]{:S(2)}, u32[]{:S(2)}) collective-permute-start(bf16[8,256,128]{2,1,0:T(8,128)(2,1)} %collective-permute-done.6.refs_3_), channel_id=1, source_target_pairs={{0,224},{16,240},{32,0},{48,16},{64,32},{80,48},{96,64},{112,80},{... | collective-permute-start | bytes 1572872 | tf_op jit(solution)/shard_map/ppermute | solution.py:29
  134.6 14.1 %collective-permute-start.13 = (bf16[4,256,128]{2,1,0:T(8,128)(2,1)S(1)}, bf16[4,256,128]{2,1,0:T(8,128)(2,1)S(1)}, u32[]{:S(2)}, u32[]{:S(2)}) collective-permute-start(bf16[4,256,128]{2,1,0:T(8,128)(2,1)S(1)} %slice.8), channel_id=1, source_target_pairs={{0,32},{16,48},{32,64},{48,80},{64,96},{80,112},{96,128},{112,144}... | collective-permute-start | bytes 786440 | tf_op jit(solution)/shard_map/ppermute | solution.py:29
  144.4 7.7 %collective-permute-start.14 = (bf16[4,256,128]{2,1,0:T(8,128)(2,1)S(1)}, bf16[4,256,128]{2,1,0:T(8,128)(2,1)S(1)}, u32[]{:S(2)}, u32[]{:S(2)}) collective-permute-start(bf16[4,256,128]{2,1,0:T(8,128)(2,1)S(1)} %slice.9), channel_id=1, source_target_pairs={{0,224},{16,240},{32,0},{48,16},{64,32},{80,48},{96,64},{112,80},{... | collective-permute-start | bytes 786440 | tf_op jit(solution)/shard_map/ppermute | solution.py:29
  148.2 13.8 %collective-permute-start.3 = (bf16[8,256,128]{2,1,0:T(8,128)(2,1)}, bf16[8,256,128]{2,1,0:T(8,128)(2,1)S(1)}, u32[]{:S(2)}, u32[]{:S(2)}) collective-permute-start(bf16[8,256,128]{2,1,0:T(8,128)(2,1)} %collective-permute-done.1.refs_2_), channel_id=1, source_target_pairs={{0,16},{16,0},{32,48},{48,32},{64,80},{80,64},{96,112},{112,96},{1... | collective-permute-start | bytes 1572872 | tf_op jit(solution)/shard_map/ppermute | solution.py:29
  148.2 14.6 %collective-permute-start.4 = (bf16[8,256,128]{2,1,0:T(8,128)(2,1)}, bf16[8,256,128]{2,1,0:T(8,128)(2,1)S(1)}, u32[]{:S(2)}, u32[]{:S(2)}) collective-permute-start(bf16[8,256,128]{2,1,0:T(8,128)(2,1)} %collective-permute-done.2.refs_3_), channel_id=1, source_target_pairs={{0,16},{16,0},{32,48},{48,32},{64,80},{80,64},{96,112},{112,96},{1... | collective-permute-start | bytes 1572872 | tf_op jit(solution)/shard_map/ppermute | solution.py:29
  148.7 15.4 %collective-permute-start.7 = (bf16[8,256,128]{2,1,0:T(8,128)(2,1)}, bf16[8,256,128]{2,1,0:T(8,128)(2,1)S(1)}, u32[]{:S(2)}, u32[]{:S(2)}) collective-permute-start(bf16[8,256,128]{2,1,0:T(8,128)(2,1)} %collective-permute-done.5.refs_2_), channel_id=1, source_target_pairs={{0,16},{16,0},{32,48},{48,32},{64,80},{80,64},{96,112},{112,96},{1... | collective-permute-start | bytes 1572872 | tf_op jit(solution)/shard_map/ppermute | solution.py:29
  152.1 38.4 %collective-permute-start.15 = (bf16[8,256,128]{2,1,0:T(8,128)(2,1)}, bf16[8,256,128]{2,1,0:T(8,128)(2,1)}, u32[]{:S(2)}, u32[]{:S(2)}) collective-permute-start(bf16[8,256,128]{2,1,0:T(8,128)(2,1)} %bitcast.4.refs_2_), channel_id=1, source_target_pairs={{0,16},{16,0},{32,48},{48,32},{64,80},{80,64},{96,112},{112,96},{1... | collective-permute-start | bytes 1572872 | tf_op jit(solution)/shard_map/ppermute | solution.py:29
  152.8 24.1 %collective-permute-start.8 = (bf16[8,256,128]{2,1,0:T(8,128)(2,1)}, bf16[8,256,128]{2,1,0:T(8,128)(2,1)}, u32[]{:S(2)}, u32[]{:S(2)}) collective-permute-start(bf16[8,256,128]{2,1,0:T(8,128)(2,1)} %collective-permute-done.6.refs_3_), channel_id=1, source_target_pairs={{0,16},{16,0},{32,48},{48,32},{64,80},{80,64},{96,112},{112,96},{1... | collective-permute-start | bytes 1572872 | tf_op jit(solution)/shard_map/ppermute | solution.py:29
  162.8 19.3 %collective-permute-start.11 = (bf16[8,256,128]{2,1,0:T(8,128)(2,1)}, bf16[8,256,128]{2,1,0:T(8,128)(2,1)}, u32[]{:S(2)}, u32[]{:S(2)}) collective-permute-start(bf16[8,256,128]{2,1,0:T(8,128)(2,1)} %collective-permute-done.9.refs_2_), channel_id=1, source_target_pairs={{0,16},{16,0},{32,48},{48,32},{64,80},{80,64},{96,112},{112,96},{1... | collective-permute-start | bytes 1572872 | tf_op jit(solution)/shard_map/ppermute | solution.py:29
  163.6 21.3 %collective-permute-start.12 = (bf16[8,256,128]{2,1,0:T(8,128)(2,1)}, bf16[8,256,128]{2,1,0:T(8,128)(2,1)}, u32[]{:S(2)}, u32[]{:S(2)}) collective-permute-start(bf16[8,256,128]{2,1,0:T(8,128)(2,1)} %collective-permute-done.10.refs_3_), channel_id=1, source_target_pairs={{0,16},{16,0},{32,48},{48,32},{64,80},{80,64},{96,112},{112,96},{1... | collective-permute-start | bytes 1572872 | tf_op jit(solution)/shard_map/ppermute | solution.py:29
  164.9 25.5 %collective-permute-start.16 = (bf16[8,256,128]{2,1,0:T(8,128)(2,1)}, bf16[8,256,128]{2,1,0:T(8,128)(2,1)}, u32[]{:S(2)}, u32[]{:S(2)}) collective-permute-start(bf16[8,256,128]{2,1,0:T(8,128)(2,1)} %constant_dynamic-update-slice_fusion.refs_3_), channel_id=1, source_target_pairs={{0,16},{16,0},{32,48},{48,32},{64,80},{80,64},{96,112},{112,96},{1... | collective-permute-start | bytes 1572872 | tf_op jit(solution)/shard_map/ppermute | solution.py:29
  164.9 7.9 %copy-start.7 = (bf16[8,256,128]{2,1,0:T(8,128)(2,1)S(1)}, bf16[8,256,128]{2,1,0:T(8,128)(2,1)}, u32[]{:S(2)}) copy-start(bf16[8,256,128]{2,1,0:T(8,128)(2,1)} %copy-done.6) | copy-start | bytes 1572868
  164.9 7.9 %copy-start.9 = (bf16[8,256,128]{2,1,0:T(8,128)(2,1)S(1)}, bf16[8,256,128]{2,1,0:T(8,128)(2,1)}, u32[]{:S(2)}) copy-start(bf16[8,256,128]{2,1,0:T(8,128)(2,1)} %copy-done.8) | copy-start | bytes 1572868
  171.2 1.7 copy-start.1
  172.8 5.1 %copy-start.5 = (bf16[8,256,128]{2,1,0:T(8,128)(2,1)S(1)}, bf16[8,256,128]{2,1,0:T(8,128)(2,1)}, u32[]{:S(2)}) copy-start(bf16[8,256,128]{2,1,0:T(8,128)(2,1)} %copy-done.4) | copy-start | bytes 1572868
  177.0 20.6 %collective-permute-start.17 = (bf16[4,96,256]{2,1,0:T(8,128)(2,1)S(1)}, bf16[4,96,256]{2,1,0:T(8,128)(2,1)S(1)}, u32[]{:S(2)}, u32[]{:S(2)}) collective-permute-start(bf16[4,96,256]{2,1,0:T(8,128)(2,1)S(1)} %get-tuple-element.23), channel_id=1, source_target_pairs={{0,1},{16,17},{32,33},{48,49},{64,65},{80,81},{96,97},{112,113},{1... | collective-permute-start | bytes 589832 | tf_op jit(solution)/shard_map/ppermute | solution.py:29
  182.1 15.5 %collective-permute-start.18 = (bf16[4,96,256]{2,1,0:T(8,128)(2,1)S(1)}, bf16[4,96,256]{2,1,0:T(8,128)(2,1)S(1)}, u32[]{:S(2)}, u32[]{:S(2)}) collective-permute-start(bf16[4,96,256]{2,1,0:T(8,128)(2,1)S(1)} %get-tuple-element.24), channel_id=1, source_target_pairs={{0,1},{16,17},{32,33},{48,49},{64,65},{80,81},{96,97},{112,113},{1... | collective-permute-start | bytes 589832 | tf_op jit(solution)/shard_map/ppermute | solution.py:29
  189.3 8.6 %collective-permute-start.19 = (bf16[4,96,256]{2,1,0:T(8,128)(2,1)S(1)}, bf16[4,96,256]{2,1,0:T(8,128)(2,1)S(1)}, u32[]{:S(2)}, u32[]{:S(2)}) collective-permute-start(bf16[4,96,256]{2,1,0:T(8,128)(2,1)S(1)} %get-tuple-element.25), channel_id=1, source_target_pairs={{0,1},{16,17},{32,33},{48,49},{64,65},{80,81},{96,97},{112,113},{1... | collective-permute-start | bytes 589832 | tf_op jit(solution)/shard_map/ppermute | solution.py:29
  194.8 8.1 %collective-permute-start.20 = (bf16[4,96,256]{2,1,0:T(8,128)(2,1)S(1)}, bf16[4,96,256]{2,1,0:T(8,128)(2,1)S(1)}, u32[]{:S(2)}, u32[]{:S(2)}) collective-permute-start(bf16[4,96,256]{2,1,0:T(8,128)(2,1)S(1)} %get-tuple-element.26), channel_id=1, source_target_pairs={{0,1},{16,17},{32,33},{48,49},{64,65},{80,81},{96,97},{112,113},{1... | collective-permute-start | bytes 589832 | tf_op jit(solution)/shard_map/ppermute | solution.py:29
  (3 other events, 2.4 us)
